TPU v7x, 512 devices: a whole 4x8x8 slice. The times are simulated.
512 devices in a mesh: group: 32 (over y, x), dev: 16 (over z, core).
Axes of the slice: x: 4, y: 8, z: 8, core: 2. Of those that a mesh axis runs over, the one named last changes fastest.
Arguments:
- tokens: bfloat16 [4096, 3584], P('group', 'dev'), may hold values from -6 to 6
- upstream: bfloat16 [4096, 3584], P('group', 'dev'), may hold values from -6 to 6
- route_probs: float32 [4096, 4], P('group'), may hold values from 0.05 to 1
- expert_ids: int32 [4096, 4], P('group'), may hold values from 0 to 31, all different within a row; in each aligned block of 128 rows (0 to 127, 128 to 255, ...) at most 18 rows name the same one
- w_gate: bfloat16 [32, 3584, 2048], P('group', None, 'dev'), may hold values from -0.09375 to 0.09375
- w_up: bfloat16 [32, 3584, 2048], P('group', None, 'dev'), may hold values from -0.09375 to 0.09375
- w_down: bfloat16 [32, 2048, 3584], P('group', 'dev'), may hold values from -0.125 to 0.125
Outputs:
- grad_tokens: bfloat16 [4096, 3584], P('group', 'dev')
- grad_probs: float32 [4096, 4], P('group')
Inputs may be any that keep to these rules, and one draw needn't show every extreme that they name: `expert_ids`: in each block of 128 tokens (one index of group) no expert is named by more than 18 routes, a bound that some block reaches; a token's experts differ.
All inputs are finite; a program needn't handle non-finite values.
Results may differ from a plain program's by a relative error of at most 0.024.
Values may be sent and summed in bfloat16 or wider, within the bound.
A program may use at most 64 MiB of HBM per device.

v0:
```python
import jax
import jax.numpy as jnp
from jax import lax
from jax.sharding import PartitionSpec as P


def local_slots(expert_ids, experts, capacity):
    flat = expert_ids.reshape(-1)
    onehot = (flat[:, None] == jnp.arange(experts, dtype=jnp.int32)).astype(jnp.int32)
    before = jnp.cumsum(onehot, axis=0) - onehot
    place = jnp.sum(before * onehot, axis=-1)
    return flat * capacity + place


def on_device(tokens, upstream, route_probs, expert_ids, w_gate, w_up, w_down):
    tok_g, width_dev = tokens.shape
    top = expert_ids.shape[1]
    experts = lax.axis_size("group")
    capacity = tok_g * top * 9 // (8 * experts)
    routes = tok_g * top
    slot = local_slots(expert_ids, experts, capacity)
    table = (
        jnp.full((experts * capacity,), routes, jnp.int32)
        .at[slot]
        .set(jnp.arange(routes, dtype=jnp.int32))
    )
    owner = jnp.where(table < routes, table // top, tok_g)
    flat_probs = jnp.concatenate([route_probs.reshape(-1), jnp.zeros((1,), jnp.float32)])
    tok_ext = jnp.concatenate([tokens, jnp.zeros((1, width_dev), jnp.bfloat16)])
    grad_ext = jnp.concatenate([upstream, jnp.zeros((1, width_dev), jnp.bfloat16)])
    send_x = tok_ext[owner].reshape(experts, capacity, width_dev)
    send_dy = (flat_probs[table][:, None] * grad_ext[owner].astype(jnp.float32)).astype(
        jnp.bfloat16
    )
    send_dy = send_dy.reshape(experts, capacity, width_dev)
    recv_x, recv_dy = (
        lax.all_to_all(send_x, "group", split_axis=0, concat_axis=0, tiled=True),
        lax.all_to_all(send_dy, "group", split_axis=0, concat_axis=0, tiled=True),
    )
    rows_e = experts * capacity
    recv_x = recv_x.reshape(rows_e, width_dev)
    recv_dy = recv_dy.reshape(rows_e, width_dev)
    wgate = w_gate[0]
    wup = w_up[0]
    wdown = w_down[0]
    part_x = lax.all_gather(recv_x, "dev", axis=1, tiled=True)
    part_dy = lax.all_gather(recv_dy, "dev", axis=1, tiled=True)
    gate = jnp.dot(part_x, wgate, preferred_element_type=jnp.float32)
    upper = jnp.dot(part_x, wup, preferred_element_type=jnp.float32)
    back = lax.dot_general(
        part_dy, wdown, (((1,), (1,)), ((), ())), preferred_element_type=jnp.float32
    )
    gate, upper, back = (gate, upper, back)
    sig = jax.nn.sigmoid(gate)
    act = gate * sig
    slope = sig * (1.0 + gate * (1.0 - sig))
    score_part = jnp.sum(act * upper * back, axis=-1)
    score = lax.psum(score_part, "dev")
    score_home = lax.all_to_all(
        score.reshape(experts, capacity), "group", split_axis=0, concat_axis=0, tiled=True
    )
    grad_probs = score_home.reshape(-1)[slot].reshape(tok_g, top) / route_probs
    d_gate = (back * upper * slope).astype(jnp.bfloat16)
    d_up = (back * act).astype(jnp.bfloat16)
    contract = (((1,), (1,)), ((), ()))
    term = lax.dot_general(d_gate, wgate, contract, preferred_element_type=jnp.float32)
    term = term + lax.dot_general(d_up, wup, contract, preferred_element_type=jnp.float32)
    summed = lax.psum_scatter(
        term.astype(jnp.bfloat16), "dev", scatter_dimension=1, tiled=True
    ).astype(jnp.float32)
    home_rows = lax.all_to_all(
        summed.reshape(experts, capacity, width_dev).astype(jnp.bfloat16),
        "group",
        split_axis=0,
        concat_axis=0,
        tiled=True,
    ).astype(jnp.float32)
    per_route = home_rows.reshape(rows_e, width_dev)[slot].reshape(tok_g, top, width_dev)
    grad_tokens = jnp.sum(per_route, axis=1).astype(jnp.bfloat16)
    return (grad_tokens, grad_probs)


def solution(mesh):
    placed = (
        P("group", "dev"),
        P("group", "dev"),
        P("group", None),
        P("group", None),
        P("group", None, "dev"),
        P("group", None, "dev"),
        P("group", "dev", None),
    )
    return jax.shard_map(
        on_device,
        mesh=mesh,
        in_specs=placed,
        out_specs=(P("group", "dev"), P("group", None)),
        check_vma=False,
    )
```

profile of v0, /device:TPU:1, one launch (start us, length us, event | category | flops | bytes accessed | tf_op | source)
XLA Modules:
  0.0 238.7 jit_solution(8567598840951257729)
XLA Ops:
  7.2 0.8 broadcast_multiply_fusion
  8.0 0.8 copy.24
  9.2 1.2 reduce-window.6
  10.8 2.4 %scatter_custom_fusion = s32[576]{0:T(1024)S(1)} fusion(s32[512]{0:T(512)S(1)} %bitcast.41, s32[512]{0:T(512)S(1)} %iota.11, s32[]{:T(128)} %constant.16.clone.1), kind=kCustom, calls=%fused_computation.47 | custom fusion | bytes 2308 | tf_op jit(solution)/shard_map/scatter | solution.py:25
  13.3 0.9 copy.29
  14.2 2.7 %gather_fusion.2 = bf16[576,224]{1,0:T(8,128)(2,1)S(1)} fusion(bf16[129,224]{1,0:T(8,128)(2,1)S(1)} %concatenate.11, s32[1024]{0:T(1024)S(1)} %get-tuple-element.10), kind=kCustom, calls=%fused_computation.2 | custom fusion | bytes 518400 | tf_op jit(solution)/shard_map/gather | solution.py:31
  17.1 24.1 %all_to_all.24 = bf16[32,18,224]{2,1,0:T(8,128)(2,1)S(1)} all-to-all(bf16[32,18,224]{2,1,0:T(8,128)(2,1)S(1)} %reshape.97), channel_id=1, replica_groups=mesh['group'=32,'dev'=16] {'group'}, dimensions={0} | all-to-all | bytes 516096 | tf_op jit(solution)/shard_map/all_to_all | solution.py:37
  41.4 0.9 copy.30
  42.6 2.6 %gather_fusion = f32[576]{0:T(1024)S(1)} fusion(f32[513]{0:T(1024)S(1)} %pad_maximum_fusion, s32[1024]{0:T(1024)S(1)} %get-tuple-element.11), kind=kCustom, calls=%fused_computation | custom fusion | bytes 6912 | tf_op jit(solution)/shard_map/gather | solution.py:32
  45.4 2.7 %gather_fusion.1 = bf16[576,224]{1,0:T(8,128)(2,1)S(1)} fusion(bf16[129,224]{1,0:T(8,128)(2,1)S(1)} %concatenate.10, s32[1024]{0:T(1024)S(1)} %get-tuple-element.10), kind=kCustom, calls=%fused_computation.1 | custom fusion | bytes 518400 | tf_op jit(solution)/shard_map/gather | solution.py:32
  48.4 17.8 %all_to_all.25 = bf16[32,18,224]{2,1,0:T(8,128)(2,1)S(1)} all-to-all(bf16[32,18,224]{2,1,0:T(8,128)(2,1)S(1)} %multiply_convert_fusion), channel_id=1, replica_groups=mesh['group'=32,'dev'=16] {'group'}, dimensions={0} | all-to-all | bytes 516096 | tf_op jit(solution)/shard_map/all_to_all | solution.py:38
  66.4 0.9 copy.28
  67.5 21.9 %all-gather.5.cloned.1.call-done = bf16[576,3584]{0,1:T(8,128)(2,1)} async-done(((bf16[576,224]{0,1:T(8,128)(2,1)}), bf16[576,3584]{0,1:T(8,128)(2,1)}) %all-gather.5.cloned.1.call-update) | async-done | bytes 4128784 | tf_op jit(solution)/shard_map/all_gather | solution.py:46
  89.5 3.8 %fusion.2 = f32[576,128]{1,0:T(8,128)S(1)} fusion(bf16[576,3584]{0,1:T(8,128)(2,1)} %all-gather.5.cloned.1.call-done, bf16[1,3584,128]{2,1,0:T(8,128)(2,1)S(1)} %copy-done), kind=kOutput, calls=%fused_computation.9 | convolution fusion | flops 528482304 | bytes 5341184 | tf_op jit(solution)/shard_map/dot_general | solution.py:48
  93.3 1.4 fusion.5
  94.7 40.9 %all-gather.3.cloned.1.call-done = bf16[576,3584]{0,1:T(8,128)(2,1)} async-done(((bf16[576,224]{0,1:T(8,128)(2,1)}), bf16[576,3584]{0,1:T(8,128)(2,1)}) %all-gather.3.cloned.1.call-update) | async-done | bytes 4128784 | tf_op jit(solution)/shard_map/all_gather | solution.py:47
  135.6 3.8 %multiply_reduce_fusion = (f32[576]{0:T(1024)S(1)}, f32[576,128]{1,0:T(8,128)S(1)}) fusion(f32[576,128]{1,0:T(8,128)S(1)} %fusion.5, f32[576,128]{1,0:T(8,128)S(1)} %fusion.2, bf16[576,3584]{0,1:T(8,128)(2,1)} %all-gather.3.cloned.1.call-done, bf16[1,128,3584]{2,1,0:T(8,128)(2,1)S(1)} %copy-done.5), kind=kOutput, calls=%fused_computation.17 | convolution fusion | flops 528997824 | bytes 5933312 | tf_op jit(solution)/shard_map/dot_general | solution.py:50
  139.4 1.4 fusion
  140.8 3.5 %add_convert_fusion = bf16[576,3584]{0,1:T(8,128)(2,1)} fusion(f32[576,3584]{0,1:T(8,128)S(1)} %fusion, bf16[1,3584,128]{2,1,0:T(8,128)(2,1)S(1)} %copy-done.2, f32[576,128]{1,0:T(8,128)S(1)} %get-tuple-element.9, f32[576,128]{1,0:T(8,128)S(1)} %fusion.2), kind=kOutput, calls=%fused_computation.6 | convolution fusion | flops 533053440 | bytes 13893632 | tf_op jit(solution)/shard_map/dot_general | solution.py:67
  144.5 44.2 %psum.7 = f32[32,1,18]{2,0,1:T(8,128)} all-reduce(f32[32,1,18]{2,0,1:T(8,128)S(1)} %all_to_all.18), channel_id=1, replica_groups=mesh['group'=32,'dev'=16] {'dev'}, use_global_device_ids=true, to_apply=%region_7.8 | all-reduce | flops 576 | bytes 4608 | tf_op jit(solution)/shard_map/psum | solution.py:58
  188.7 9.2 %all-to-all-start.3 = ((f32[32,1,18]{2,1,0:T(1,128)}), f32[32,1,18]{2,1,0:T(1,128)S(1)}, u32[]{:S(2)}, u32[]{:S(2)}) async-start(f32[32,1,18]{2,1,0:T(1,128)} %bitcast.6), calls=%async_computation.4 | async-start | bytes 32768 | tf_op jit(solution)/shard_map/all_to_all | solution.py:59
  197.9 8.1 %reduce-scatter.2.cloned.1.call-done = bf16[576,224]{0,1:T(8,128)(2,1)} async-done(((bf16[576,3584]{0,1:T(8,128)(2,1)}), bf16[576,224]{0,1:T(8,128)(2,1)}) %reduce-scatter.2.cloned.1.call-update) | async-done | bytes 258064 | tf_op jit(solution)/shard_map/reduce_scatter | solution.py:68
  206.1 1.1 copy.31
  207.2 0.8 convert_element_type.44
  208.0 9.6 %all-to-all-start.2 = ((bf16[32,18,224]{2,1,0:T(8,128)(2,1)}), bf16[32,18,224]{2,1,0:T(8,128)(2,1)S(1)}, u32[]{:S(2)}, u32[]{:S(2)}) async-start(bf16[32,18,224]{2,1,0:T(8,128)(2,1)} %convert_element_type.44), calls=%async_computation.3 | async-start | bytes 786432 | tf_op jit(solution)/shard_map/all_to_all | solution.py:71
  217.6 0.5 broadcast.115
  218.2 0.7 reduce.5
  219.0 2.3 gather_fusion.4
  221.4 0.7 copy.35
  222.0 7.1 %all-to-all-done.2 = bf16[32,18,224]{2,1,0:T(8,128)(2,1)S(1)} async-done(((bf16[32,18,224]{2,1,0:T(8,128)(2,1)}), bf16[32,18,224]{2,1,0:T(8,128)(2,1)S(1)}, u32[]{:S(2)}, u32[]{:S(2)}) %all-to-all-start.2) | async-done | bytes 258080 | tf_op jit(solution)/shard_map/all_to_all | solution.py:71
  229.3 1.6 gather_fusion.3
  231.4 0.7 copy.34
  (52 shorter events, 3.3 us)
Async XLA Ops:
  7.2 82.3 %copy-start = (bf16[1,3584,128]{2,1,0:T(8,128)(2,1)S(1)}, bf16[1,3584,128]{2,1,0:T(8,128)(2,1)}, u32[]{:S(2)}) copy-start(bf16[1,3584,128]{2,1,0:T(8,128)(2,1)} %param.11) | copy-start | bytes 2752516
  7.2 35.1 %copy-start.4 = (f32[128,4]{0,1:T(4,128)S(1)}, f32[128,4]{0,1:T(4,128)}, u32[]{:S(2)}) copy-start(f32[128,4]{0,1:T(4,128)} %param.9) | copy-start | bytes 6148
  7.2 82.3 %all-gather.5.cloned.1.call-start = ((), (), s32[]{:S(2)}) async-start(), calls=%async_computation.6 | async-start | bytes 4874240 | tf_op jit(solution)/shard_map/all_gather | solution.py:46
  14.2 31.0 %copy-start.3 = (bf16[128,224]{0,1:T(8,128)(2,1)S(1)}, bf16[128,224]{0,1:T(8,128)(2,1)}, u32[]{:S(2)}) copy-start(bf16[128,224]{0,1:T(8,128)(2,1)} %param.8) | copy-start | bytes 172036
  42.3 93.3 %all-gather.3.cloned.1.call-start = ((), (), s32[]{:S(2)}) async-start(), calls=%async_computation.5 | async-start | bytes 4874240 | tf_op jit(solution)/shard_map/all_gather | solution.py:47
  48.2 45.1 %copy-start.2 = (bf16[1,3584,128]{2,1,0:T(8,128)(2,1)S(1)}, bf16[1,3584,128]{2,1,0:T(8,128)(2,1)}, u32[]{:S(2)}) copy-start(bf16[1,3584,128]{2,1,0:T(8,128)(2,1)} %param.12) | copy-start | bytes 2752516
  67.3 68.3 %copy-start.5 = (bf16[1,128,3584]{2,1,0:T(8,128)(2,1)S(1)}, bf16[1,128,3584]{2,1,0:T(8,128)(2,1)}, u32[]{:S(2)}) copy-start(bf16[1,128,3584]{2,1,0:T(8,128)(2,1)} %param.13) | copy-start | bytes 2752516
  67.3 138.8 %reduce-scatter.2.cloned.1.call-start = ((), (), s32[]{:S(2)}) async-start(), calls=%async_computation.7 | async-start | bytes 4874240 | tf_op jit(solution)/shard_map/reduce_scatter | solution.py:68
  89.4 3.9 %copy-start.1 = (bf16[576,3584]{0,1:T(8,128)(2,1)S(1)}, bf16[576,3584]{0,1:T(8,128)(2,1)}, u32[]{:S(2)}) copy-start(bf16[576,3584]{0,1:T(8,128)(2,1)} %all-gather.5.cloned.1.call-done) | copy-start | bytes 12386308
  188.7 19.3 %all-to-all-start.3 = ((f32[32,1,18]{2,1,0:T(1,128)}), f32[32,1,18]{2,1,0:T(1,128)S(1)}, u32[]{:S(2)}, u32[]{:S(2)}) async-start(f32[32,1,18]{2,1,0:T(1,128)} %bitcast.6), calls=%async_computation.4 | async-start | bytes 32768 | tf_op jit(solution)/shard_map/all_to_all | solution.py:59
  208.0 21.2 %all-to-all-start.2 = ((bf16[32,18,224]{2,1,0:T(8,128)(2,1)}), bf16[32,18,224]{2,1,0:T(8,128)(2,1)S(1)}, u32[]{:S(2)}, u32[]{:S(2)}) async-start(bf16[32,18,224]{2,1,0:T(8,128)(2,1)} %convert_element_type.44), calls=%async_computation.3 | async-start | bytes 786432 | tf_op jit(solution)/shard_map/all_to_all | solution.py:71
Sparse Core Ops, SparseCore 0:
  42.4 47.0 all-gather.4
  91.6 43.9 all-gather.2
  144.5 61.5 reduce-scatter.1
where the time goes:
time: 242 us; the launch traced here: 239 us
  blocking collectives  86.2 us (36%)
  waiting for transfers between devices  78.1 us (32%)
  local copies, waits for them, and re-layouts  23.9 us (10%)
  starting transfers between devices  19.1 us (8%)
  between operations  14.1 us (6%)
  matrix products  14 us (6%)
  other arithmetic  3.34 us (1%)
    psum x1, blocking collectives, on_device(): score = lax.psum(score_part, 'dev')  44.2 us
    all_gather x1, waiting for transfers between devices, on_device(): part_dy = lax.all_gather(recv_dy, 'dev', axis=1, tiled=True)  40.9 us
    all_to_all x1, blocking collectives, on_device(): lax.all_to_all(send_x, 'group', split_axis=0, concat_axis=0, tiled=True)  24.1 us
    all_gather x1, waiting for transfers between devices, on_device(): part_x = lax.all_gather(recv_x, 'dev', axis=1, tiled=True)  21.9 us
    all_to_all x1, blocking collectives, on_device(): lax.all_to_all(send_dy, 'group', split_axis=0, concat_axis=0, tiled=True)  17.8 us
    all_to_all x1, starting transfers between devices, on_device(): lax.all_to_all(summed.reshape(experts, capacity, width_dev).astype(jnp.bf...  9.61 us
    all_to_all x1, starting transfers between devices, on_device(): lax.all_to_all(score.reshape(experts, capacity), 'group', split_axis=0, c...  9.23 us
    reduce_scatter x1, waiting for transfers between devices, on_device(): lax.psum_scatter(term.astype(jnp.bfloat16), 'dev', scatter_dimension=1, t...  8.12 us
  transfers between devices with their start and end apart: 5, of which 4 were waited for; matrix products, arithmetic and copies ran while one was open for 8% of the time, Pallas kernels for 0%

commit v1 on v0

v1 whole, which is shorter than its diff:
```python
import functools

import jax
import jax.numpy as jnp
from jax import lax
from jax.experimental import pallas as pl
from jax.experimental.pallas import tpu as pltpu
from jax.sharding import PartitionSpec as P

BF16 = jnp.bfloat16
F32 = jnp.float32
I32 = jnp.int32
MESH = pl.DeviceIdType.MESH

NX = 4
MAIN = 16
CAP = 18
WIDE = 512
BACK = 256


def iota(shape, axis):
    return lax.broadcasted_iota(I32, shape, axis)


def flag(mask):
    return jnp.where(mask, 1.0, 0.0).astype(BF16)


def dot(a, b):
    return lax.dot_general(a, b, (((1,), (0,)), ((), ())), preferred_element_type=F32)


def dot_nt(a, b):
    return lax.dot_general(a, b, (((1,), (1,)), ((), ())), preferred_element_type=F32)


def dot_tn(a, b):
    return lax.dot_general(a, b, (((0,), (0,)), ((), ())), preferred_element_type=F32)


def kernel(
    ny,
    nz,
    x_ref,
    u_ref,
    prob_ref,
    ids_ref,
    wg_hbm,
    wu_hbm,
    wd_hbm,
    out_ref,
    gp_ref,
    tt,
    snd,
    rcv,
    place,
    hits,
    pick,
    pick2,
    ag,
    wgu,
    wdraw,
    wdt,
    acc_gu,
    acc_b,
    dgu,
    rs_snd,
    rs_rcv,
    scores,
    ret_snd,
    ret_rcv,
    load_sem,
    swap_send,
    swap_recv,
    fwd_send,
    fwd_recv,
    ag_send,
    ag_recv,
    rs_send,
    rs_recv,
    sc_send,
    sc_recv,
    ret_send,
    ret_recv,
):
    feats, toks = x_ref.shape
    top = ids_ref.shape[0]
    hid = wd_hbm.shape[0]
    wide_d = wd_hbm.shape[1]
    ngroup = ny * NX
    nslot = ngroup // 2
    nb = nslot // 2
    main = nb * MAIN
    rows = nb * CAP
    chunk = 2 * feats
    pad = WIDE - chunk

    g = lax.axis_index("group")
    d = lax.axis_index("dev")
    y, x = lax.div(g, NX), lax.rem(g, NX)
    z, c = lax.div(d, 2), lax.rem(d, 2)
    sib = {"group": g, "dev": z * 2 + 1 - c}

    def target(n):
        p, dx = lax.div(n, NX), lax.rem(n, NX)
        e = lax.rem(y + p + ny - 1, ny) * NX + lax.rem(x + dx, NX)
        return p, dx, e

    def home_of(s):
        p, dx = lax.div(s, 2), 2 * lax.rem(s, 2) + c
        h = lax.rem(y + ny + ny - (p + ny - 1), ny) * NX + lax.rem(x + NX - dx, NX)
        return p, dx, h

    barrier = pltpu.get_barrier_semaphore()

    def greet(n, carry):
        p, dx, e = target(n)
        own = jnp.logical_and(n == NX, c == 0)

        @pl.when(jnp.logical_not(own))
        def _():
            pl.semaphore_signal(
                barrier, inc=1, device_id={"group": e, "dev": z * 2 + lax.rem(dx, 2)}, device_id_type=MESH
            )

        @pl.when(lax.rem(dx, 2) == c)
        def _():
            pl.semaphore_signal(barrier, inc=1, device_id={"group": e, "dev": z * 2 + 1 - c}, device_id_type=MESH)

        return carry

    lax.fori_loop(0, ngroup, greet, 0)

    def greet_z(k, carry):
        pl.semaphore_signal(
            barrier, inc=1, device_id={"group": g, "dev": lax.rem(z + k, nz) * 2 + c}, device_id_type=MESH
        )
        return carry

    lax.fori_loop(1, nz, greet_z, 0)
    greeted = ngroup + nslot + nz - 1 - (1 - c)

    loads = [
        pltpu.make_async_copy(wd_hbm, wdraw, load_sem.at[0]),
        pltpu.make_async_copy(wg_hbm, wgu.at[pl.ds(0, wide_d), pl.ds(0, hid)], load_sem.at[1]),
        pltpu.make_async_copy(wu_hbm, wgu.at[pl.ds(0, wide_d), pl.ds(2 * hid, hid)], load_sem.at[2]),
    ]
    for copy in loads:
        copy.start()

    zero = jnp.zeros((pad, toks), BF16)
    tt[0, pl.ds(0, feats), :] = x_ref[...]
    tt[0, pl.ds(feats, feats), :] = u_ref[...]
    tt[0, pl.ds(chunk, pad), :] = zero
    tt[1, pl.ds(0, pad), :] = zero
    tt[1, pl.ds(pad, feats), :] = x_ref[...]
    tt[1, pl.ds(pad + feats, feats), :] = u_ref[...]

    n_col = iota((ngroup, 1), 0)
    p_col = lax.shift_right_logical(n_col, 2)
    dx_col = jnp.bitwise_and(n_col, NX - 1)
    e_col = jnp.bitwise_and(y + p_col + ny - 1, ny - 1) * NX + jnp.bitwise_and(x + dx_col, NX - 1)
    ids = ids_ref[...]
    probs = prob_ref[...]
    hit = jnp.zeros((ngroup, toks), F32)
    prob_n = jnp.zeros((ngroup, toks), F32)
    for k in range(top):
        same = jnp.broadcast_to(ids[k : k + 1, :], (ngroup, toks)) == jnp.broadcast_to(e_col, (ngroup, toks))
        hit = hit + jnp.where(same, 1.0, 0.0)
        prob_n = prob_n + jnp.where(same, jnp.broadcast_to(probs[k : k + 1, :], (ngroup, toks)), 0.0)
    earlier = flag(iota((toks, toks), 0) < iota((toks, toks), 1))
    place_n = jnp.where(hit > 0.5, dot(hit.astype(BF16), earlier), -1.0)
    hits[...] = place_n
    place_bf = place_n.astype(BF16)
    part1 = prob_n.astype(BF16)
    rest = prob_n - part1.astype(F32)
    part2 = rest.astype(BF16)
    part3 = (rest - part2.astype(F32)).astype(BF16)

    step_rows = min(8, ngroup) * MAIN

    def fill(i, carry):
        base = pl.multiple_of(i * step_rows, step_rows)
        row = iota((step_rows, 1), 0)
        rr = jnp.bitwise_and(row, MAIN - 1)
        spread = flag(lax.shift_right_logical(base + iota((step_rows, ngroup), 0), 4) == iota((step_rows, ngroup), 1))
        at = dot(spread, place_bf)
        pr = dot(spread, part1) + dot(spread, part2) + dot(spread, part3)
        m1 = at == jnp.broadcast_to(rr.astype(F32), at.shape)
        m2 = at == jnp.broadcast_to((MAIN + jnp.bitwise_and(rr, 1)).astype(F32), at.shape)
        pick1 = flag(m1)
        pickx = flag(m2)
        pick[pl.ds(base, step_rows), :] = pick1
        pick2[pl.ds(base, step_rows), :] = pickx
        pr1 = jnp.sum(jnp.where(m1, pr, 0.0), axis=1, keepdims=True)
        pr2 = jnp.sum(jnp.where(m2, pr, 0.0), axis=1, keepdims=True)
        got = dot_nt(pick1, tt[0])
        lane = iota((step_rows, WIDE), 1)
        got = jnp.where(jnp.logical_and(lane >= feats, lane < chunk), got * pr1, got)
        odd = dot_nt(pickx, tt[0])
        even = dot_nt(pickx, tt[1])
        part = lax.shift_right_logical(rr, 1)
        extra = jnp.zeros((step_rows, 128), F32)
        for tile in range(WIDE // 128):
            cut = slice(tile * 128, tile * 128 + 128)
            extra = jnp.where(part == 2 * tile, even[:, cut], extra)
            extra = jnp.where(part == 2 * tile + 1, odd[:, cut], extra)
        lane = iota((step_rows, 128), 1)
        extra = jnp.where(part * pad + lane - (128 - pad) >= feats, extra * pr2, extra)
        snd[pl.ds(base, step_rows), pl.ds(0, WIDE - 128)] = got[:, : WIDE - 128].astype(BF16)
        snd[pl.ds(base, step_rows), pl.ds(WIDE - 128, 128)] = jnp.where(
            lane >= 128 - pad, extra, got[:, WIDE - 128 :]
        ).astype(BF16)
        return carry

    lax.fori_loop(0, ngroup * MAIN // step_rows, fill, 0)

    pl.semaphore_wait(barrier, greeted)

    def fwd_copy(n, b, sem):
        p, dx, e = target(n)
        slot = p * 2 + lax.div(dx, 2) - b * nb
        return pltpu.make_async_remote_copy(
            src_ref=snd.at[pl.ds(pl.multiple_of(n * MAIN, MAIN), MAIN), :],
            dst_ref=rcv.at[b, c, pl.ds(pl.multiple_of(slot * MAIN, MAIN), MAIN), :],
            send_sem=sem,
            recv_sem=fwd_recv.at[b],
            device_id={"group": e, "dev": z * 2 + lax.rem(dx, 2)},
            device_id_type=MESH,
        )

    own_b, own_slot = (0, NX // 2) if ny > 2 else (1, 0)

    for b in range(2):

        def send_rows(n, carry, b=b):
            @pl.when(n != NX)
            def _():
                fwd_copy(n, b, fwd_send.at[0]).start()

            return carry

        lax.fori_loop(b * nslot, (b + 1) * nslot, send_rows, 0)
        if b == own_b:

            @pl.when(c == 0)
            def _():
                pltpu.make_async_copy(
                    snd.at[pl.ds(NX * MAIN, MAIN), :],
                    rcv.at[own_b, 0, pl.ds(own_slot * MAIN, MAIN), :],
                    fwd_recv.at[own_b],
                ).start()

            @pl.when(c == 1)
            def _():
                fwd_copy(NX, own_b, fwd_send.at[1]).start()

    swaps = [
        pltpu.make_async_remote_copy(
            src_ref=wg_hbm,
            dst_ref=wgu.at[pl.ds(0, wide_d), pl.ds(hid, hid)],
            send_sem=swap_send.at[0],
            recv_sem=swap_recv.at[0],
            device_id=sib,
            device_id_type=MESH,
        ),
        pltpu.make_async_remote_copy(
            src_ref=wu_hbm,
            dst_ref=wgu.at[pl.ds(0, wide_d), pl.ds(3 * hid, hid)],
            send_sem=swap_send.at[1],
            recv_sem=swap_recv.at[1],
            device_id=sib,
            device_id_type=MESH,
        ),
        pltpu.make_async_remote_copy(
            src_ref=wdt.at[pl.ds(pad, wide_d), pl.ds(0, hid)],
            dst_ref=wdt.at[pl.ds(pad, wide_d), pl.ds(hid, hid)],
            send_sem=swap_send.at[2],
            recv_sem=swap_recv.at[2],
            device_id=sib,
            device_id_type=MESH,
        ),
    ]
    swaps[0].start()
    swaps[1].start()

    loads[0].wait()

    def turn(i, carry):
        base = pl.multiple_of(i * 128, 128)
        wdt[pl.ds(pl.multiple_of(base + pad, pad), 128), pl.ds(0, hid)] = wdraw[:, pl.ds(base, 128)].T
        return carry

    lax.fori_loop(0, wide_d // 128, turn, 0)
    swaps[2].start()

    wgu[pl.ds(wide_d, pad), :] = jnp.zeros((pad, 4 * hid), BF16)
    wdt[pl.ds(0, pad), :] = jnp.zeros((pad, 2 * hid), BF16)
    acc_gu[...] = jnp.zeros_like(acc_gu)
    acc_b[...] = jnp.zeros_like(acc_b)

    def set_place(i, carry):
        base = pl.multiple_of(i * 128, 128)
        a = base + iota((128, 2 * chunk), 0)
        f = iota((128, 2 * chunk), 1)
        goal = a + jnp.where(a >= feats, feats, 0)
        keep = a < chunk
        place[0, pl.ds(base, 128), :] = flag(jnp.logical_and(keep, f == goal))
        place[1, pl.ds(base, 128), :] = flag(jnp.logical_and(keep, f == goal + feats))
        return carry

    lax.fori_loop(0, WIDE // 128, set_place, 0)

    def build(b):
        pltpu.make_async_copy(rcv.at[b], rcv.at[b], fwd_recv.at[b]).wait()
        widen = flag(iota((128, WIDE), 0) == 128 - pad + jnp.bitwise_and(iota((128, WIDE), 1), pad - 1))
        mine = lax.shift_right_logical(jnp.bitwise_and(iota((main, WIDE), 0), MAIN - 1), 1) == lax.shift_right_logical(
            iota((main, WIDE), 1), pad.bit_length() - 1
        )
        a, r = iota((2 * nb, main), 0), iota((2 * nb, main), 1)
        gather = flag(
            jnp.logical_and(
                lax.shift_right_logical(a, 1) == lax.shift_right_logical(r, 4),
                jnp.bitwise_and(a, 1) == jnp.bitwise_and(r, 1),
            )
        )
        whole, extra = 0.0, 0.0
        for h in range(2):
            got = rcv[b, h]
            wide = jnp.where(mine, dot(got[:, WIDE - 128 :], widen), 0.0).astype(BF16)
            last = dot(gather, wide).astype(BF16)
            whole = whole + dot(got, place[h])
            extra = extra + dot(last, place[h])
        ag[b, z, pl.ds(0, main), :] = whole.astype(BF16)
        ag[b, z, pl.ds(main, 2 * nb), :] = extra.astype(BF16)

    right = {"group": g, "dev": lax.rem(z + 1, nz) * 2 + c}
    left = {"group": g, "dev": lax.rem(z + nz - 1, nz) * 2 + c}
    half = nz // 2
    hops = [[half, nz - 1 - half], [nz - 1 - half, half]]

    def ag_copy(b, way, s):
        which = lax.rem(z + nz - s, nz) if way == 0 else lax.rem(z + s, nz)
        return pltpu.make_async_remote_copy(
            src_ref=ag.at[b, which],
            dst_ref=ag.at[b, which],
            send_sem=ag_send.at[b, way, s],
            recv_sem=ag_recv.at[b, way, s],
            device_id=right if way == 0 else left,
            device_id_type=MESH,
        )

    def multiply(b, which):
        lane = iota((rows, 128), 1)
        mid = ag[b, which, :, pl.ds(WIDE - 128, 128)]
        none = jnp.zeros_like(mid)
        first = jnp.concatenate(
            [ag[b, which, :, pl.ds(0, WIDE - 128)], jnp.where(lane < 128 - pad, mid, none)], axis=1
        )
        second = jnp.concatenate(
            [jnp.where(lane >= 128 - pad, mid, none), ag[b, which, :, pl.ds(WIDE, WIDE - 128)]], axis=1
        )
        at = pl.ds(pl.multiple_of(which * chunk, pad), WIDE)
        acc_gu[b] += dot(first, wgu[at, :])
        acc_b[b] += dot(second, wdt[at, :])

    for b in range(2):
        build(b)
        for way in range(2):
            if hops[b][way] > 0:
                ag_copy(b, way, 0).start()

    loads[1].wait()
    loads[2].wait()
    for copy in swaps:
        copy.wait_recv()

    def arrive(b, s):
        for way in range(2):
            if s < hops[b][way]:
                ag_copy(b, way, s).wait_recv()
                if s + 1 < hops[b][way]:
                    ag_copy(b, way, s + 1).start()
        for way in range(2):
            if s < hops[b][way]:
                multiply(b, lax.rem(z + nz - s - 1, nz) if way == 0 else lax.rem(z + s + 1, nz))

    for b in range(2):
        multiply(b, z)
    for s in range(half):
        for b in range(2):
            arrive(b, s)
            if s == half - 1:
                finish = functools.partial(middle, b, hid, acc_gu, acc_b, dgu)
                row = finish()
                if b == 0:
                    scores[z] = jnp.zeros(scores.shape[1:], F32)
                    scores[z, pl.ds(0, 4), pl.ds(0, rows)] = row[0:4]
                else:
                    scores[z, pl.ds(4, 4), pl.ds(0, rows)] = row[4:8]
                rs_step(b, 0, z, nz, hops, rows, chunk, pad, dgu, wgu, rs_snd, rs_rcv, rs_send, rs_recv, right, left)

    def sc_copy(k):
        return pltpu.make_async_remote_copy(
            src_ref=scores.at[z],
            dst_ref=scores.at[z],
            send_sem=sc_send.at[k],
            recv_sem=sc_recv.at[k],
            device_id={"group": g, "dev": lax.rem(z + k, nz) * 2 + c},
            device_id_type=MESH,
        )

    for k in range(1, nz):
        sc_copy(k).start()

    for s in range(1, half):
        for b in range(2):
            rs_step(b, s, z, nz, hops, rows, chunk, pad, dgu, wgu, rs_snd, rs_rcv, rs_send, rs_recv, right, left)

    for k in range(1, nz):
        sc_copy(k).wait_recv()
    score = scores[0]
    for k in range(1, nz):
        score = score + scores[k]

    def ret_copy(b, i, h, sem):
        p, dx, home = home_of(b * nb + i)
        n = p * NX + dx
        return pltpu.make_async_remote_copy(
            src_ref=ret_snd.at[b, h, pl.ds(pl.multiple_of(i * MAIN, MAIN), MAIN), :],
            dst_ref=ret_rcv.at[pl.ds(pl.multiple_of(n * MAIN, MAIN), MAIN), :],
            send_sem=sem,
            recv_sem=ret_recv.at[b],
            device_id={"group": home, "dev": z * 2 + h},
            device_id_type=MESH,
        )

    for b in range(2):
        total = dot_nt(dgu[b], wgu[pl.ds(pl.multiple_of(z * chunk, pad), WIDE), :])
        for way in range(2):
            if hops[b][way] > 0:
                s = hops[b][way] - 1
                rs_copy(b, way, s, z, nz, hops, rs_snd, rs_rcv, rs_send, rs_recv, right, left).wait_recv()
                total = total + rs_rcv[b, way, s].astype(F32)
        total = total.astype(BF16)
        whole, extra = total[:main], total[main:]

        row = iota((main, BACK), 0)
        lane = iota((main, BACK), 1)
        q = jnp.bitwise_and(row, MAIN - 1)
        value = jnp.broadcast_to(score[4 * b : 4 * b + 1, :], (main, BACK))
        upper = value.astype(BF16).astype(F32)
        lower = value - upper
        slot = jnp.where(lane < main, lax.shift_right_logical(lane, 4), lax.shift_right_logical(lane - main, 1))
        fits = jnp.logical_and(lax.shift_right_logical(row, 4) == slot, lane < rows)
        value = jnp.where(q == MAIN - 2, upper, jnp.where(q == MAIN - 1, lower, 0.0))
        value = jnp.where(fits, value, 0.0).astype(BF16)
        a, l = iota((BACK, BACK), 0), iota((BACK, BACK), 1)
        number = jnp.where(a < main, jnp.bitwise_and(a, MAIN - 1), MAIN + jnp.bitwise_and(a, 1))
        carried = dot(value, flag(l == feats + number))

        again = flag(
            jnp.logical_and(
                lax.shift_right_logical(iota((main, 2 * nb), 0), 4)
                == lax.shift_right_logical(iota((main, 2 * nb), 1), 1),
                jnp.bitwise_and(iota((main, 2 * nb), 0), 1) == jnp.bitwise_and(iota((main, 2 * nb), 1), 1),
            )
        )
        extra = dot(again, extra)
        room = BACK - feats
        for h in range(2):
            a, l = iota((WIDE, BACK), 0), iota((WIDE, BACK), 1)
            shift = flag(jnp.logical_and(a == l + feats * h, l < feats))
            rel = a - feats * h
            inside = jnp.logical_and(rel >= 0, rel < feats)
            tail = flag(jnp.logical_and(inside, jnp.bitwise_and(a, room - 1) == l - feats))
            lane = iota((main, WIDE), 1) - feats * h
            rr = lax.shift_right_logical(jnp.bitwise_and(iota((main, WIDE), 0), MAIN - 1), 1)
            mine = jnp.logical_and(lane >= rr * room, lane < rr * room + room)
            ends = jnp.where(jnp.logical_and(mine, lane < feats), extra, 0.0).astype(BF16)
            ret_snd[b, h] = (dot(whole, shift) + dot(ends, tail) + carried).astype(BF16)

        def send_back(i, carry, b=b):
            for h in range(2):
                own = jnp.logical_and(c == 0, i == own_slot) if (b == own_b and h == 0) else None
                if own is None:
                    ret_copy(b, i, h, ret_send.at[0]).start()
                else:

                    @pl.when(jnp.logical_not(own))
                    def _():
                        ret_copy(b, i, h, ret_send.at[0]).start()

            return carry

        lax.fori_loop(0, nb, send_back, 0)
        if b == own_b:

            @pl.when(c == 0)
            def _():
                pltpu.make_async_copy(
                    ret_snd.at[own_b, 0, pl.ds(own_slot * MAIN, MAIN), :],
                    ret_rcv.at[pl.ds(NX * MAIN, MAIN), :],
                    ret_recv.at[own_b],
                ).start()

    room = BACK - feats
    n_rows = nslot * MAIN
    total = 0.0
    sums = []
    for b in range(2):
        part = pl.ds(b * n_rows, n_rows)
        pltpu.make_async_copy(ret_rcv.at[part], ret_rcv.at[part], ret_recv.at[b]).wait()
        got = ret_rcv[part, :]
        end = got[:, BACK - 128 :]
        widen = flag(iota((128, BACK), 0) == 128 - room + jnp.bitwise_and(iota((128, BACK), 1), room - 1))
        mine = lax.shift_right_logical(
            jnp.bitwise_and(iota((n_rows, BACK), 0), MAIN - 1), 1
        ) == lax.shift_right_logical(iota((n_rows, BACK), 1), room.bit_length() - 1)
        wide = jnp.where(mine, dot(end, widen), 0.0).astype(BF16)
        total = total + dot_tn(got, pick[part, :]) + dot_tn(wide, pick2[part, :])
        a, r = iota((nslot, n_rows), 0), iota((nslot, n_rows), 1)
        this = a == lax.shift_right_logical(r, 4)
        r = jnp.bitwise_and(r, MAIN - 1)
        sums.append(
            dot(flag(jnp.logical_and(this, r == MAIN - 2)), end)
            + dot(flag(jnp.logical_and(this, r == MAIN - 1)), end)
        )
    out_ref[...] = total[:feats].astype(BF16)

    at = hits[...]
    score = jnp.concatenate(sums, axis=0)
    found = jnp.zeros((ngroup, toks), F32)
    for q in range(CAP):
        col = 128 - room + q
        found = jnp.where(at == float(q), jnp.broadcast_to(score[:, col : col + 1], found.shape), found)
    ids = ids_ref[...]
    for k in range(top):
        same = jnp.broadcast_to(ids[k : k + 1, :], (ngroup, toks)) == jnp.broadcast_to(e_col, (ngroup, toks))
        value = jnp.sum(jnp.where(same, found, 0.0), axis=0, keepdims=True)
        gp_ref[pl.ds(k, 1), :] = value / prob_ref[pl.ds(k, 1), :]

    most = 2 * nslot - 1
    part = snd.at[pl.ds(0, most * MAIN), :]
    pltpu.make_async_copy(part, part, fwd_send.at[0]).wait()
    for copy in swaps:
        copy.wait_send()
    for b in range(2):
        for way in range(2):
            for s in range(hops[b][way]):
                ag_copy(b, way, s).wait_send()
                rs_copy(b, way, s, z, nz, hops, rs_snd, rs_rcv, rs_send, rs_recv, right, left).wait_send()
    for k in range(1, nz):
        sc_copy(k).wait_send()
    part = ret_rcv.at[pl.ds(0, most * MAIN), :]
    pltpu.make_async_copy(part, part, ret_send.at[0]).wait()

    @pl.when(c == 1)
    def _():
        one = snd.at[pl.ds(0, MAIN), :]
        pltpu.make_async_copy(one, one, fwd_send.at[1]).wait()
        one = ret_rcv.at[pl.ds(0, MAIN), :]
        pltpu.make_async_copy(one, one, ret_send.at[0]).wait()


def middle(b, hid, acc_gu, acc_b, dgu):
    gate, upper = acc_gu[b, :, pl.ds(0, 2 * hid)], acc_gu[b, :, pl.ds(2 * hid, 2 * hid)]
    back = acc_b[b]
    sig = 1.0 / (1.0 + jnp.exp(-gate))
    act = gate * sig
    slope = sig * (1.0 + gate * (1.0 - sig))
    dgu[b, :, pl.ds(0, 2 * hid)] = (back * upper * slope).astype(BF16)
    dgu[b, :, pl.ds(2 * hid, 2 * hid)] = (back * act).astype(BF16)
    prod = act * upper * back
    return lax.dot_general(
        jnp.ones((8, 2 * hid), F32),
        prod,
        (((1,), (1,)), ((), ())),
        preferred_element_type=F32,
        precision=lax.Precision.HIGHEST,
    )


def rs_copy(b, way, s, z, nz, hops, rs_snd, rs_rcv, rs_send, rs_recv, right, left):
    return pltpu.make_async_remote_copy(
        src_ref=rs_snd.at[b, way, s],
        dst_ref=rs_rcv.at[b, way, s],
        send_sem=rs_send.at[b, way, s],
        recv_sem=rs_recv.at[b, way, s],
        device_id=right if way == 0 else left,
        device_id_type=MESH,
    )


def rs_step(b, s, z, nz, hops, rows, chunk, pad, dgu, wgu, rs_snd, rs_rcv, rs_send, rs_recv, right, left):
    for way in range(2):
        if s < hops[b][way]:
            left_over = hops[b][way] - s
            which = lax.rem(z + left_over, nz) if way == 0 else lax.rem(z + nz - left_over, nz)
            total = dot_nt(dgu[b], wgu[pl.ds(pl.multiple_of(which * chunk, pad), WIDE), :])
            if s > 0:
                rs_copy(b, way, s - 1, z, nz, hops, rs_snd, rs_rcv, rs_send, rs_recv, right, left).wait_recv()
                total = total + rs_rcv[b, way, s - 1].astype(F32)
            rs_snd[b, way, s] = total.astype(BF16)
            rs_copy(b, way, s, z, nz, hops, rs_snd, rs_rcv, rs_send, rs_recv, right, left).start()


def on_device(ny, nz, tokens, upstream, route_probs, expert_ids, w_gate, w_up, w_down):
    toks, feats = tokens.shape
    top = expert_ids.shape[1]
    wide_d, hid = w_gate.shape[1], w_gate.shape[2]
    ngroup = ny * NX
    nslot = ngroup // 2
    nb = nslot // 2
    main, rows = nb * MAIN, nb * CAP
    chunk = 2 * feats
    pad = WIDE - chunk
    half = nz // 2
    dma = pltpu.SemaphoreType.DMA
    vmem = pl.BlockSpec(memory_space=pltpu.VMEM)
    hbm = pl.BlockSpec(memory_space=pl.ANY)
    out, gp = pl.pallas_call(
        functools.partial(kernel, ny, nz),
        out_shape=(jax.ShapeDtypeStruct((feats, toks), BF16), jax.ShapeDtypeStruct((top, toks), F32)),
        in_specs=[vmem] * 4 + [hbm] * 3,
        out_specs=(vmem, vmem),
        scratch_shapes=[
            pltpu.VMEM((2, WIDE, toks), BF16),
            pltpu.VMEM((ngroup * MAIN, WIDE), BF16),
            pltpu.VMEM((2, 2, main, WIDE), BF16),
            pltpu.VMEM((2, WIDE, 2 * chunk), BF16),
            pltpu.VMEM((ngroup, toks), F32),
            pltpu.VMEM((ngroup * MAIN, toks), BF16),
            pltpu.VMEM((ngroup * MAIN, toks), BF16),
            pltpu.VMEM((2, nz, rows, 2 * chunk), BF16),
            pltpu.VMEM((wide_d + pad, 4 * hid), BF16),
            pltpu.VMEM((hid, wide_d), BF16),
            pltpu.VMEM((wide_d + pad, 2 * hid), BF16),
            pltpu.VMEM((2, rows, 4 * hid), F32),
            pltpu.VMEM((2, rows, 2 * hid), F32),
            pltpu.VMEM((2, rows, 4 * hid), BF16),
            pltpu.VMEM((2, 2, half, rows, WIDE), BF16),
            pltpu.VMEM((2, 2, half, rows, WIDE), BF16),
            pltpu.VMEM((nz, 8, BACK), F32),
            pltpu.VMEM((2, 2, main, BACK), BF16),
            pltpu.VMEM((ngroup * MAIN, BACK), BF16),
            dma((3,)),
            dma((3,)),
            dma((3,)),
            dma((2,)),
            dma((2,)),
            dma((2, 2, half)),
            dma((2, 2, half)),
            dma((2, 2, half)),
            dma((2, 2, half)),
            dma((nz,)),
            dma((nz,)),
            dma((1,)),
            dma((2,)),
        ],
        compiler_params=pltpu.CompilerParams(
            collective_id=0, has_side_effects=True, vmem_limit_bytes=48 * 1024 * 1024
        ),
    )(tokens.T, upstream.T, route_probs.T, expert_ids.T, w_gate[0], w_up[0], w_down[0])
    return out.T, gp.T


def solution(mesh):
    ny = mesh.shape["group"] // NX
    nz = mesh.shape["dev"] // 2
    placed = (
        P("group", "dev"),
        P("group", "dev"),
        P("group", None),
        P("group", None),
        P("group", None, "dev"),
        P("group", None, "dev"),
        P("group", "dev", None),
    )
    return jax.shard_map(
        functools.partial(on_device, ny, nz),
        mesh=mesh,
        in_specs=placed,
        out_specs=(P("group", "dev"), P("group", None)),
        check_vma=False,
    )
```

time: 242 us -> 114 us (0.47); the launches traced: 239 us -> 114 us
  Pallas kernels: 0 us -> 106 us
  blocking collectives: 86.2 us -> 0 us
  waiting for transfers between devices: 78.1 us -> 0 us
  starting transfers between devices: 19.1 us -> 0 us
  local copies, waits for them, and re-layouts: 23.9 us -> 7.06 us
  matrix products: 14 us -> 0 us
  between operations: 14.1 us -> 0.66 us
  other arithmetic: 3.34 us -> 0 us
    pallas_call x0 -> x1, Pallas kernels: none -> 106 us  [on_device(): pl.pallas_call(functools.partial(kernel, ny, nz), out_shape=(jax.ShapeDty...]
    all_gather x2 -> x0, waiting for transfers between devices: 62.8 us -> none  [the longest x1 40.9 us: on_device(): part_dy = lax.all_gather(recv_dy, 'dev', axis=1, tiled=True)]
    psum x1 -> x0, blocking collectives: 44.2 us -> none  [on_device(): score = lax.psum(score_part, 'dev')]
    all_to_all x2 -> x0, blocking collectives: 41.9 us -> none  [the longest x1 24.1 us: on_device(): lax.all_to_all(send_x, 'group', split_axis=0, concat_axis=0, tiled=True)]
    all_to_all x2 -> x0, starting transfers between devices: 18.8 us -> none  [the longest x1 9.61 us: on_device(): lax.all_to_all(summed.reshape(experts, capacity, width_dev).astype(jnp.bf...]
    dot_general x5 -> x0, matrix products: 14 us -> none  [the longest x1 3.83 us: on_device(): gate = jnp.dot(part_x, wgate, preferred_element_type=jnp.float32)]
    gather x5 -> x0, local copies, waits for them, and re-layouts: 11.9 us -> none  [the longest x1 2.73 us: on_device(): send_x = tok_ext[owner].reshape(experts, capacity, width_dev)]
    reduce_scatter x1 -> x0, waiting for transfers between devices: 8.12 us -> none  [on_device(): lax.psum_scatter(term.astype(jnp.bfloat16), 'dev', scatter_dimension=1, t...]
  transfers between devices with their start and end apart: 5 -> 0, of which waited for: 4 -> 0; matrix products, arithmetic and copies ran while one was open for 8% -> 0% of each run, Pallas kernels for 0% -> 0%
where the time goes in v1:
time: 114 us
  Pallas kernels  106 us (93%)
  local copies, waits for them, and re-layouts  7.06 us (6%)
    pallas_call x1, Pallas kernels, on_device(): pl.pallas_call(functools.partial(kernel, ny, nz), out_shape=(jax.ShapeDty...  106 us
    unnamed x16, local copies, waits for them, and re-layouts  7.06 us

profile of v1, /device:TPU:1, one launch (start us, length us, event | category | flops | bytes accessed | tf_op | source)
XLA Modules:
  0.0 114.0 jit_solution(462785942226165673)
XLA Ops:
  0.6 0.0 copy-start.6
  0.6 0.0 copy-start.5
  0.7 0.7 copy-done.6
  1.3 0.0 copy-done.5
  1.3 0.0 copy-start
  1.3 1.2 %copy-done = bf16[1,3584,128]{2,1,0:T(8,128)(2,1)S(1)} copy-done((bf16[1,3584,128]{2,1,0:T(8,128)(2,1)S(1)}, bf16[1,3584,128]{2,1,0:T(8,128)(2,1)}, u32[]{:S(2)}) %copy-start) | copy-done | bytes 917528
  2.5 0.0 copy-start.1
  2.5 1.2 %copy-done.1 = bf16[1,3584,128]{2,1,0:T(8,128)(2,1)S(1)} copy-done((bf16[1,3584,128]{2,1,0:T(8,128)(2,1)S(1)}, bf16[1,3584,128]{2,1,0:T(8,128)(2,1)}, u32[]{:S(2)}) %copy-start.1) | copy-done | bytes 917528
  3.7 0.0 copy-start.2
  3.7 1.2 %copy-done.2 = bf16[1,128,3584]{2,1,0:T(8,128)(2,1)S(1)} copy-done((bf16[1,128,3584]{2,1,0:T(8,128)(2,1)S(1)}, bf16[1,128,3584]{2,1,0:T(8,128)(2,1)}, u32[]{:S(2)}) %copy-start.2) | copy-done | bytes 917528
  4.9 0.0 copy-start.3
  4.9 0.8 copy-done.3
  5.7 0.0 copy-start.4
  5.7 0.8 copy-done.4
  6.5 106.3 %shard_map.86 = (bf16[224,128]{1,0:T(8,128)(2,1)S(1)}, f32[4,128]{1,0:T(4,128)S(1)}) custom-call(bf16[224,128]{1,0:T(8,128)(2,1)S(1)} %bitcast.13, bf16[224,128]{1,0:T(8,128)(2,1)S(1)} %bitcast.14, f32[4,128]{1,0:T(4,128)S(1)} %bitcast.16, s32[4,128]{1,0:T(4,128)S(1)} %bitcast.17, bf16[3584,128]{1,0:T(8,128)(2,1)S(1)} %bitcast.9, ...), custom_call_target="tpu_custom_call" | custom-call | tf_op jit(solution)/shard_map/pallas_call | solution.py:623
  112.8 0.6 copy.11
  113.4 0.6 copy.12
Async XLA Ops:
  0.6 0.7 copy-start.6
  0.6 0.7 copy-start.5
  1.3 1.2 %copy-start = (bf16[1,3584,128]{2,1,0:T(8,128)(2,1)S(1)}, bf16[1,3584,128]{2,1,0:T(8,128)(2,1)}, u32[]{:S(2)}) copy-start(bf16[1,3584,128]{2,1,0:T(8,128)(2,1)} %param.11) | copy-start | bytes 2752516
  2.5 1.2 %copy-start.1 = (bf16[1,3584,128]{2,1,0:T(8,128)(2,1)S(1)}, bf16[1,3584,128]{2,1,0:T(8,128)(2,1)}, u32[]{:S(2)}) copy-start(bf16[1,3584,128]{2,1,0:T(8,128)(2,1)} %param.12) | copy-start | bytes 2752516
  3.7 1.2 %copy-start.2 = (bf16[1,128,3584]{2,1,0:T(8,128)(2,1)S(1)}, bf16[1,128,3584]{2,1,0:T(8,128)(2,1)}, u32[]{:S(2)}) copy-start(bf16[1,128,3584]{2,1,0:T(8,128)(2,1)} %param.13) | copy-start | bytes 2752516
  4.9 0.8 copy-start.3
  5.7 0.8 copy-start.4

commit v2 on v1

--- a/solution.py
+++ b/solution.py
@@ -42,19 +42,22 @@
 def kernel(
     ny,
     nz,
-    x_ref,
-    u_ref,
-    prob_ref,
-    ids_ref,
+    x_hbm,
+    u_hbm,
+    prob_hbm,
+    ids_hbm,
     wg_hbm,
     wu_hbm,
     wd_hbm,
     out_ref,
     gp_ref,
+    ids_ref,
+    prob_ref,
     tt,
     snd,
     rcv,
     place,
+    away,
     hits,
     pick,
     pick2,
@@ -84,8 +87,8 @@
     ret_send,
     ret_recv,
 ):
-    feats, toks = x_ref.shape
-    top = ids_ref.shape[0]
+    feats, toks = x_hbm.shape
+    top = ids_hbm.shape[0]
     hid = wd_hbm.shape[0]
     wide_d = wd_hbm.shape[1]
     ngroup = ny * NX
@@ -112,6 +115,20 @@
         h = lax.rem(y + ny + ny - (p + ny - 1), ny) * NX + lax.rem(x + NX - dx, NX)
         return p, dx, h
 
+    loads = [
+        pltpu.make_async_copy(ids_hbm, ids_ref, load_sem.at[0]),
+        pltpu.make_async_copy(prob_hbm, prob_ref, load_sem.at[1]),
+        pltpu.make_async_copy(x_hbm, tt.at[0, pl.ds(0, feats), :], load_sem.at[2]),
+        pltpu.make_async_copy(u_hbm, tt.at[0, pl.ds(feats, feats), :], load_sem.at[3]),
+        pltpu.make_async_copy(x_hbm, tt.at[1, pl.ds(pad, feats), :], load_sem.at[4]),
+        pltpu.make_async_copy(u_hbm, tt.at[1, pl.ds(pad + feats, feats), :], load_sem.at[5]),
+        pltpu.make_async_copy(wd_hbm, wdraw, load_sem.at[6]),
+        pltpu.make_async_copy(wg_hbm, wgu.at[pl.ds(0, wide_d), pl.ds(0, hid)], load_sem.at[7]),
+        pltpu.make_async_copy(wu_hbm, wgu.at[pl.ds(0, wide_d), pl.ds(2 * hid, hid)], load_sem.at[8]),
+    ]
+    for copy in loads:
+        copy.start()
+
     barrier = pltpu.get_barrier_semaphore()
 
     def greet(n, carry):
@@ -141,26 +158,16 @@
     lax.fori_loop(1, nz, greet_z, 0)
     greeted = ngroup + nslot + nz - 1 - (1 - c)
 
-    loads = [
-        pltpu.make_async_copy(wd_hbm, wdraw, load_sem.at[0]),
-        pltpu.make_async_copy(wg_hbm, wgu.at[pl.ds(0, wide_d), pl.ds(0, hid)], load_sem.at[1]),
-        pltpu.make_async_copy(wu_hbm, wgu.at[pl.ds(0, wide_d), pl.ds(2 * hid, hid)], load_sem.at[2]),
-    ]
-    for copy in loads:
-        copy.start()
-
     zero = jnp.zeros((pad, toks), BF16)
-    tt[0, pl.ds(0, feats), :] = x_ref[...]
-    tt[0, pl.ds(feats, feats), :] = u_ref[...]
     tt[0, pl.ds(chunk, pad), :] = zero
     tt[1, pl.ds(0, pad), :] = zero
-    tt[1, pl.ds(pad, feats), :] = x_ref[...]
-    tt[1, pl.ds(pad + feats, feats), :] = u_ref[...]
 
     n_col = iota((ngroup, 1), 0)
     p_col = lax.shift_right_logical(n_col, 2)
     dx_col = jnp.bitwise_and(n_col, NX - 1)
     e_col = jnp.bitwise_and(y + p_col + ny - 1, ny - 1) * NX + jnp.bitwise_and(x + dx_col, NX - 1)
+    loads[0].wait()
+    loads[1].wait()
     ids = ids_ref[...]
     probs = prob_ref[...]
     hit = jnp.zeros((ngroup, toks), F32)
@@ -178,7 +185,7 @@
     part2 = rest.astype(BF16)
     part3 = (rest - part2.astype(F32)).astype(BF16)
 
-    step_rows = min(8, ngroup) * MAIN
+    step_rows = min(8, ngroup // 2) * MAIN
 
     def fill(i, carry):
         base = pl.multiple_of(i * step_rows, step_rows)
@@ -214,8 +221,10 @@
         ).astype(BF16)
         return carry
 
-    lax.fori_loop(0, ngroup * MAIN // step_rows, fill, 0)
-
+    for copy in loads[2:6]:
+        copy.wait()
+    steps = ngroup * MAIN // step_rows
+    lax.fori_loop(0, steps // 2, fill, 0)
     pl.semaphore_wait(barrier, greeted)
 
     def fwd_copy(n, b, sem):
@@ -232,9 +241,8 @@
 
     own_b, own_slot = (0, NX // 2) if ny > 2 else (1, 0)
 
-    for b in range(2):
-
-        def send_rows(n, carry, b=b):
+    def send_batch(b):
+        def send_rows(n, carry):
             @pl.when(n != NX)
             def _():
                 fwd_copy(n, b, fwd_send.at[0]).start()
@@ -255,6 +263,9 @@
             @pl.when(c == 1)
             def _():
                 fwd_copy(NX, own_b, fwd_send.at[1]).start()
+
+    send_batch(0)
+    lax.fori_loop(steps // 2, steps, fill, 0)
 
     swaps = [
         pltpu.make_async_remote_copy(
@@ -285,7 +296,7 @@
     swaps[0].start()
     swaps[1].start()
 
-    loads[0].wait()
+    loads[6].wait()
 
     def turn(i, carry):
         base = pl.multiple_of(i * 128, 128)
@@ -312,6 +323,15 @@
 
     lax.fori_loop(0, WIDE // 128, set_place, 0)
 
+    room = BACK - feats
+
+    def set_away(h, carry):
+        a, l = iota((WIDE, BACK), 0) - feats * h, iota((WIDE, BACK), 1)
+        away[h, pl.ds(0, WIDE), :] = flag(jnp.logical_and(a == l, l < feats))
+        inside = jnp.logical_and(a >= 0, a < feats)
+        away[h, pl.ds(WIDE, WIDE), :] = flag(jnp.logical_and(inside, jnp.bitwise_and(a, room - 1) == l - feats))
+        return carry
+
     def build(b):
         pltpu.make_async_copy(rcv.at[b], rcv.at[b], fwd_recv.at[b]).wait()
         widen = flag(iota((128, WIDE), 0) == 128 - pad + jnp.bitwise_and(iota((128, WIDE), 1), pad - 1))
@@ -365,41 +385,77 @@
         acc_gu[b] += dot(first, wgu[at, :])
         acc_b[b] += dot(second, wdt[at, :])
 
-    for b in range(2):
-        build(b)
-        for way in range(2):
-            if hops[b][way] > 0:
-                ag_copy(b, way, 0).start()
-
-    loads[1].wait()
-    loads[2].wait()
-    for copy in swaps:
-        copy.wait_recv()
-
-    def arrive(b, s):
-        for way in range(2):
-            if s < hops[b][way]:
-                ag_copy(b, way, s).wait_recv()
-                if s + 1 < hops[b][way]:
-                    ag_copy(b, way, s + 1).start()
-        for way in range(2):
-            if s < hops[b][way]:
-                multiply(b, lax.rem(z + nz - s - 1, nz) if way == 0 else lax.rem(z + s + 1, nz))
-
-    for b in range(2):
-        multiply(b, z)
-    for s in range(half):
-        for b in range(2):
-            arrive(b, s)
-            if s == half - 1:
-                finish = functools.partial(middle, b, hid, acc_gu, acc_b, dgu)
-                row = finish()
-                if b == 0:
-                    scores[z] = jnp.zeros(scores.shape[1:], F32)
-                    scores[z, pl.ds(0, 4), pl.ds(0, rows)] = row[0:4]
-                else:
-                    scores[z, pl.ds(4, 4), pl.ds(0, rows)] = row[4:8]
-                rs_step(b, 0, z, nz, hops, rows, chunk, pad, dgu, wgu, rs_snd, rs_rcv, rs_send, rs_recv, right, left)
+    def ag_wait(b, way, s):
+        if s < hops[b][way]:
+            ag_copy(b, way, s).wait_recv()
+
+    def ag_start(b, way, s):
+        if s < hops[b][way]:
+            ag_copy(b, way, s).start()
+
+    def ag_use(b, way, s):
+        if s < hops[b][way]:
+            multiply(b, lax.rem(z + nz - s - 1, nz) if way == 0 else lax.rem(z + s + 1, nz))
+
+    def rs_copy(b, way, s):
+        return pltpu.make_async_remote_copy(
+            src_ref=rs_snd.at[b, way, s],
+            dst_ref=rs_rcv.at[b, way, s],
+            send_sem=rs_send.at[b, way, s],
+            recv_sem=rs_recv.at[b, way, s],
+            device_id=right if way == 0 else left,
+            device_id_type=MESH,
+        )
+
+    def term(b, which):
+        return dot_nt(dgu[b], wgu[pl.ds(pl.multiple_of(which * chunk, pad), WIDE), :])
+
+    tiles = WIDE // 128 - 1
+    fold = rs_snd.shape[3] - tiles * rows
+    again_at = rows - fold
+
+    def folded(total):
+        tail = total[:, tiles * 128 :]
+        lane = iota((fold, 128), 1)
+        return jnp.where(lane < pad, tail[:fold], pltpu.roll(tail[again_at:], pad, 1))
+
+    def rs_step(b, s):
+        ways = [w for w in range(2) if s < hops[b][w]]
+        totals = []
+        for way in ways:
+            over = hops[b][way] - s
+            totals.append(term(b, lax.rem(z + over, nz) if way == 0 else lax.rem(z + nz - over, nz)))
+        for way, total in zip(ways, totals):
+            tail = folded(total)
+            if s > 0:
+                rs_copy(b, way, s - 1).wait_recv()
+            for i in range(tiles + 1):
+                at = pl.ds(i * rows, rows if i < tiles else fold)
+                value = total[:, i * 128 : i * 128 + 128] if i < tiles else tail
+                if s > 0:
+                    value = value + rs_rcv[b, way, s - 1, at, :].astype(F32)
+                rs_snd[b, way, s, at, :] = value.astype(BF16)
+            rs_copy(b, way, s).start()
+
+    def middle(b):
+        gate, upper = acc_gu[b, :, pl.ds(0, 2 * hid)], acc_gu[b, :, pl.ds(2 * hid, 2 * hid)]
+        back = acc_b[b]
+        sig = 1.0 / (1.0 + jnp.exp(-gate))
+        act = gate * sig
+        slope = sig * (1.0 + gate * (1.0 - sig))
+        dgu[b, :, pl.ds(0, 2 * hid)] = (back * upper * slope).astype(BF16)
+        dgu[b, :, pl.ds(2 * hid, 2 * hid)] = (back * act).astype(BF16)
+        acc_b[b] = act * upper * back
+
+    def set_scores(b):
+        row = lax.dot_general(
+            jnp.ones((8, 2 * hid), F32),
+            acc_b[b],
+            (((1,), (1,)), ((), ())),
+            preferred_element_type=F32,
+            precision=lax.Precision.HIGHEST,
+        )
+        scores[z, pl.ds(4 * b, 4), pl.ds(0, rows)] = row[:4]
 
     def sc_copy(k):
         return pltpu.make_async_remote_copy(
@@ -411,12 +467,65 @@
             device_id_type=MESH,
         )
 
+    build(0)
+    ag_start(0, 0, 0)
+    ag_start(0, 1, 0)
+    send_batch(1)
+    scores[z] = jnp.zeros(scores.shape[1:], F32)
+    lax.fori_loop(0, 2, set_away, 0)
+    loads[7].wait()
+    loads[8].wait()
+    for copy in swaps:
+        copy.wait_recv()
+    multiply(0, z)
+
+    for s in range(half):
+        for way in range(2):
+            ag_wait(0, way, s)
+            ag_start(0, way, s + 1)
+        if s == 0:
+            ag_use(0, 0, s)
+            ag_use(0, 1, s)
+            build(1)
+        if s == max(half - 3, 0):
+            ag_start(1, 1, 0)
+        if s == max(half - 2, 0):
+            ag_start(1, 0, 0)
+        if s == 0:
+            multiply(1, z)
+        else:
+            if s == half - 1:
+                ag_wait(1, 1, 0)
+                ag_start(1, 1, 1)
+            ag_use(0, 0, s)
+            ag_use(0, 1, s)
+    if half == 1:
+        ag_wait(1, 1, 0)
+    middle(0)
+    rs_step(0, 0)
+    ag_use(1, 1, 0)
+    for i in range(half - 1):
+        ag_wait(1, 0, i)
+        ag_start(1, 0, i + 1)
+        ag_wait(1, 1, i + 1)
+        ag_start(1, 1, i + 2)
+        if i == 0:
+            set_scores(0)
+        ag_use(1, 0, i)
+        ag_use(1, 1, i + 1)
+        if i < half - 2:
+            rs_step(0, i + 1)
+    middle(1)
+    rs_step(1, 0)
+    if half > 1:
+        rs_step(0, half - 1)
+    else:
+        set_scores(0)
+    set_scores(1)
     for k in range(1, nz):
         sc_copy(k).start()
-
     for s in range(1, half):
-        for b in range(2):
-            rs_step(b, s, z, nz, hops, rows, chunk, pad, dgu, wgu, rs_snd, rs_rcv, rs_send, rs_recv, right, left)
+        rs_step(1, s)
 
     for k in range(1, nz):
         sc_copy(k).wait_recv()
@@ -437,13 +546,21 @@
         )
 
     for b in range(2):
-        total = dot_nt(dgu[b], wgu[pl.ds(pl.multiple_of(z * chunk, pad), WIDE), :])
+        total = term(b, z)
+        tail = folded(total)
+        parts = [total[:, i * 128 : i * 128 + 128] for i in range(tiles)] + [tail]
         for way in range(2):
             if hops[b][way] > 0:
                 s = hops[b][way] - 1
-                rs_copy(b, way, s, z, nz, hops, rs_snd, rs_rcv, rs_send, rs_recv, right, left).wait_recv()
-                total = total + rs_rcv[b, way, s].astype(F32)
-        total = total.astype(BF16)
+                rs_copy(b, way, s).wait_recv()
+                for i in range(tiles + 1):
+                    at = pl.ds(i * rows, rows if i < tiles else fold)
+                    parts[i] = parts[i] + rs_rcv[b, way, s, at, :].astype(F32)
+        tail = parts.pop()
+        lane = iota((rows, 128), 1)
+        tail = jnp.concatenate([tail, pltpu.roll(tail, pad, 1)[fold - again_at :]], axis=0)
+        parts.append(jnp.where(lane < pad, tail, 0.0))
+        total = jnp.concatenate([part.astype(BF16) for part in parts], axis=1)
         whole, extra = total[:main], total[main:]
 
         row = iota((main, BACK), 0)
@@ -468,18 +585,14 @@
             )
         )
         extra = dot(again, extra)
-        room = BACK - feats
         for h in range(2):
-            a, l = iota((WIDE, BACK), 0), iota((WIDE, BACK), 1)
-            shift = flag(jnp.logical_and(a == l + feats * h, l < feats))
-            rel = a - feats * h
-            inside = jnp.logical_and(rel >= 0, rel < feats)
-            tail = flag(jnp.logical_and(inside, jnp.bitwise_and(a, room - 1) == l - feats))
             lane = iota((main, WIDE), 1) - feats * h
             rr = lax.shift_right_logical(jnp.bitwise_and(iota((main, WIDE), 0), MAIN - 1), 1)
             mine = jnp.logical_and(lane >= rr * room, lane < rr * room + room)
             ends = jnp.where(jnp.logical_and(mine, lane < feats), extra, 0.0).astype(BF16)
-            ret_snd[b, h] = (dot(whole, shift) + dot(ends, tail) + carried).astype(BF16)
+            ret_snd[b, h] = (
+                dot(whole, away[h, pl.ds(0, WIDE), :]) + dot(ends, away[h, pl.ds(WIDE, WIDE), :]) + carried
+            ).astype(BF16)
 
         def send_back(i, carry, b=b):
             for h in range(2):
@@ -505,7 +618,6 @@
                     ret_recv.at[own_b],
                 ).start()
 
-    room = BACK - feats
     n_rows = nslot * MAIN
     total = 0.0
     sums = []
@@ -550,7 +662,7 @@
         for way in range(2):
             for s in range(hops[b][way]):
                 ag_copy(b, way, s).wait_send()
-                rs_copy(b, way, s, z, nz, hops, rs_snd, rs_rcv, rs_send, rs_recv, right, left).wait_send()
+                rs_copy(b, way, s).wait_send()
     for k in range(1, nz):
         sc_copy(k).wait_send()
     part = ret_rcv.at[pl.ds(0, most * MAIN), :]
@@ -562,48 +674,6 @@
         pltpu.make_async_copy(one, one, fwd_send.at[1]).wait()
         one = ret_rcv.at[pl.ds(0, MAIN), :]
         pltpu.make_async_copy(one, one, ret_send.at[0]).wait()
-
-
-def middle(b, hid, acc_gu, acc_b, dgu):
-    gate, upper = acc_gu[b, :, pl.ds(0, 2 * hid)], acc_gu[b, :, pl.ds(2 * hid, 2 * hid)]
-    back = acc_b[b]
-    sig = 1.0 / (1.0 + jnp.exp(-gate))
-    act = gate * sig
-    slope = sig * (1.0 + gate * (1.0 - sig))
-    dgu[b, :, pl.ds(0, 2 * hid)] = (back * upper * slope).astype(BF16)
-    dgu[b, :, pl.ds(2 * hid, 2 * hid)] = (back * act).astype(BF16)
-    prod = act * upper * back
-    return lax.dot_general(
-        jnp.ones((8, 2 * hid), F32),
-        prod,
-        (((1,), (1,)), ((), ())),
-        preferred_element_type=F32,
-        precision=lax.Precision.HIGHEST,
-    )
-
-
-def rs_copy(b, way, s, z, nz, hops, rs_snd, rs_rcv, rs_send, rs_recv, right, left):
-    return pltpu.make_async_remote_copy(
-        src_ref=rs_snd.at[b, way, s],
-        dst_ref=rs_rcv.at[b, way, s],
-        send_sem=rs_send.at[b, way, s],
-        recv_sem=rs_recv.at[b, way, s],
-        device_id=right if way == 0 else left,
-        device_id_type=MESH,
-    )
-
-
-def rs_step(b, s, z, nz, hops, rows, chunk, pad, dgu, wgu, rs_snd, rs_rcv, rs_send, rs_recv, right, left):
-    for way in range(2):
-        if s < hops[b][way]:
-            left_over = hops[b][way] - s
-            which = lax.rem(z + left_over, nz) if way == 0 else lax.rem(z + nz - left_over, nz)
-            total = dot_nt(dgu[b], wgu[pl.ds(pl.multiple_of(which * chunk, pad), WIDE), :])
-            if s > 0:
-                rs_copy(b, way, s - 1, z, nz, hops, rs_snd, rs_rcv, rs_send, rs_recv, right, left).wait_recv()
-                total = total + rs_rcv[b, way, s - 1].astype(F32)
-            rs_snd[b, way, s] = total.astype(BF16)
-            rs_copy(b, way, s, z, nz, hops, rs_snd, rs_rcv, rs_send, rs_recv, right, left).start()
 
 
 def on_device(ny, nz, tokens, upstream, route_probs, expert_ids, w_gate, w_up, w_down):
@@ -617,19 +687,23 @@
     chunk = 2 * feats
     pad = WIDE - chunk
     half = nz // 2
+    message = (WIDE // 128 - 1) * rows + -(-rows // 32) * 16
     dma = pltpu.SemaphoreType.DMA
     vmem = pl.BlockSpec(memory_space=pltpu.VMEM)
-    hbm = pl.BlockSpec(memory_space=pl.ANY)
+    hbm = pl.BlockSpec(memory_space=pltpu.HBM)
     out, gp = pl.pallas_call(
         functools.partial(kernel, ny, nz),
         out_shape=(jax.ShapeDtypeStruct((feats, toks), BF16), jax.ShapeDtypeStruct((top, toks), F32)),
-        in_specs=[vmem] * 4 + [hbm] * 3,
+        in_specs=[hbm] * 7,
         out_specs=(vmem, vmem),
         scratch_shapes=[
+            pltpu.VMEM((top, toks), I32),
+            pltpu.VMEM((top, toks), F32),
             pltpu.VMEM((2, WIDE, toks), BF16),
             pltpu.VMEM((ngroup * MAIN, WIDE), BF16),
             pltpu.VMEM((2, 2, main, WIDE), BF16),
             pltpu.VMEM((2, WIDE, 2 * chunk), BF16),
+            pltpu.VMEM((2, 2 * WIDE, BACK), BF16),
             pltpu.VMEM((ngroup, toks), F32),
             pltpu.VMEM((ngroup * MAIN, toks), BF16),
             pltpu.VMEM((ngroup * MAIN, toks), BF16),
@@ -640,12 +714,12 @@
             pltpu.VMEM((2, rows, 4 * hid), F32),
             pltpu.VMEM((2, rows, 2 * hid), F32),
             pltpu.VMEM((2, rows, 4 * hid), BF16),
-            pltpu.VMEM((2, 2, half, rows, WIDE), BF16),
-            pltpu.VMEM((2, 2, half, rows, WIDE), BF16),
+            pltpu.VMEM((2, 2, half, message, 128), BF16),
+            pltpu.VMEM((2, 2, half, message, 128), BF16),
             pltpu.VMEM((nz, 8, BACK), F32),
             pltpu.VMEM((2, 2, main, BACK), BF16),
             pltpu.VMEM((ngroup * MAIN, BACK), BF16),
-            dma((3,)),
+            dma((9,)),
             dma((3,)),
             dma((3,)),
             dma((2,)),
@@ -660,7 +734,7 @@
             dma((2,)),
         ],
         compiler_params=pltpu.CompilerParams(
-            collective_id=0, has_side_effects=True, vmem_limit_bytes=48 * 1024 * 1024
+            collective_id=0, has_side_effects=True, vmem_limit_bytes=60 * 1024 * 1024
         ),
     )(tokens.T, upstream.T, route_probs.T, expert_ids.T, w_gate[0], w_up[0], w_down[0])
     return out.T, gp.T

time: 114 us -> 111 us (0.974)
  local copies, waits for them, and re-layouts: 7.06 us -> 2.03 us
  Pallas kernels: 106 us -> 109 us
    unnamed x16 -> x4, local copies, waits for them, and re-layouts: 7.06 us -> 2.03 us
    pallas_call x1, Pallas kernels: 106 us -> 109 us  [on_device(): pl.pallas_call(functools.partial(kernel, ny, nz), out_shape=(jax.ShapeDty...]
where the time goes in v2:
time: 111 us
  Pallas kernels  109 us (98%)
  local copies, waits for them, and re-layouts  2.03 us (2%)
    pallas_call x1, Pallas kernels, on_device(): pl.pallas_call(functools.partial(kernel, ny, nz), out_shape=(jax.ShapeDty...  109 us

profile of v2, /device:TPU:1, one launch (start us, length us, event | category | flops | bytes accessed | tf_op | source)
XLA Modules:
  0.0 111.3 jit_solution(17596187923212581225)
XLA Ops:
  0.6 108.6 %shard_map.86 = (bf16[224,128]{1,0:T(8,128)(2,1)}, f32[4,128]{1,0:T(4,128)}) custom-call(bf16[224,128]{1,0:T(8,128)(2,1)} %bitcast.13, bf16[224,128]{1,0:T(8,128)(2,1)} %bitcast.14, f32[4,128]{1,0:T(4,128)} %bitcast.16, s32[4,128]{1,0:T(4,128)} %bitcast.17, bf16[3584,128]{1,0:T(8,128)(2,1)} %bitcast.9, bf16[3584,128]{1,0:T(8,128)(2,1)} %bitcast.10, ...), custom_call_target="tpu_custom_call" | custom-call | tf_op jit(solution)/shard_map/pallas_call | solution.py:694
  109.2 0.0 copy-start
  109.2 1.4 %copy.11 = bf16[128,224]{0,1:T(8,128)(2,1)} copy(bf16[128,224]{0,1:T(8,128)(2,1)} %bitcast.12) | data formatting | bytes 114688
  110.7 0.0 copy-done
  110.7 0.6 copy.12
Async XLA Ops:
  109.2 1.5 %copy-start = (f32[4,128]{1,0:T(4,128)S(1)}, f32[4,128]{1,0:T(4,128)}, u32[]{:S(2)}) copy-start(f32[4,128]{1,0:T(4,128)} %get-tuple-element.5) | copy-start | bytes 6148

commit v3 on v2

--- a/solution.py
+++ b/solution.py
@@ -105,15 +105,17 @@
     z, c = lax.div(d, 2), lax.rem(d, 2)
     sib = {"group": g, "dev": z * 2 + 1 - c}
 
+    ys = [lax.rem(y + k, ny) * NX for k in range(ny)]
+    xs = [lax.rem(x + k, NX) for k in range(NX)]
+    back_x = [lax.rem(x + 2 * NX - 2 * k - c, NX) for k in range(NX // 2)]
+
     def target(n):
-        p, dx = lax.div(n, NX), lax.rem(n, NX)
-        e = lax.rem(y + p + ny - 1, ny) * NX + lax.rem(x + dx, NX)
-        return p, dx, e
+        p, dx = n // NX, n % NX
+        return p, dx, ys[(p + ny - 1) % ny] + xs[dx]
 
     def home_of(s):
-        p, dx = lax.div(s, 2), 2 * lax.rem(s, 2) + c
-        h = lax.rem(y + ny + ny - (p + ny - 1), ny) * NX + lax.rem(x + NX - dx, NX)
-        return p, dx, h
+        p, k = s // 2, s % 2
+        return p * NX + 2 * k + c, ys[(1 - p) % ny] + back_x[k]
 
     loads = [
         pltpu.make_async_copy(ids_hbm, ids_ref, load_sem.at[0]),
@@ -131,31 +133,24 @@
 
     barrier = pltpu.get_barrier_semaphore()
 
-    def greet(n, carry):
+    for n in range(ngroup):
         p, dx, e = target(n)
-        own = jnp.logical_and(n == NX, c == 0)
-
-        @pl.when(jnp.logical_not(own))
-        def _():
-            pl.semaphore_signal(
-                barrier, inc=1, device_id={"group": e, "dev": z * 2 + lax.rem(dx, 2)}, device_id_type=MESH
-            )
-
-        @pl.when(lax.rem(dx, 2) == c)
-        def _():
-            pl.semaphore_signal(barrier, inc=1, device_id={"group": e, "dev": z * 2 + 1 - c}, device_id_type=MESH)
-
-        return carry
-
-    lax.fori_loop(0, ngroup, greet, 0)
-
-    def greet_z(k, carry):
+
+        def hello(e=e, core=dx % 2):
+            pl.semaphore_signal(barrier, inc=1, device_id={"group": e, "dev": z * 2 + core}, device_id_type=MESH)
+
+        if n == NX:
+            pl.when(c == 1)(hello)
+        else:
+            hello()
+    for n in range(ngroup // 2):
+        p, k = n // 2, n % 2
+        e = ys[p] + lax.rem(x + 2 * k + c, NX)
+        pl.semaphore_signal(barrier, inc=1, device_id={"group": e, "dev": z * 2 + 1 - c}, device_id_type=MESH)
+    for k in range(1, nz):
         pl.semaphore_signal(
             barrier, inc=1, device_id={"group": g, "dev": lax.rem(z + k, nz) * 2 + c}, device_id_type=MESH
         )
-        return carry
-
-    lax.fori_loop(1, nz, greet_z, 0)
     greeted = ngroup + nslot + nz - 1 - (1 - c)
 
     zero = jnp.zeros((pad, toks), BF16)
@@ -229,27 +224,22 @@
 
     def fwd_copy(n, b, sem):
         p, dx, e = target(n)
-        slot = p * 2 + lax.div(dx, 2) - b * nb
+        slot = p * 2 + dx // 2 - b * nb
         return pltpu.make_async_remote_copy(
-            src_ref=snd.at[pl.ds(pl.multiple_of(n * MAIN, MAIN), MAIN), :],
-            dst_ref=rcv.at[b, c, pl.ds(pl.multiple_of(slot * MAIN, MAIN), MAIN), :],
+            src_ref=snd.at[pl.ds(n * MAIN, MAIN), :],
+            dst_ref=rcv.at[b, c, pl.ds(slot * MAIN, MAIN), :],
             send_sem=sem,
             recv_sem=fwd_recv.at[b],
-            device_id={"group": e, "dev": z * 2 + lax.rem(dx, 2)},
+            device_id={"group": e, "dev": z * 2 + dx % 2},
             device_id_type=MESH,
         )
 
     own_b, own_slot = (0, NX // 2) if ny > 2 else (1, 0)
 
     def send_batch(b):
-        def send_rows(n, carry):
-            @pl.when(n != NX)
-            def _():
+        for n in range(b * nslot, (b + 1) * nslot):
+            if n != NX:
                 fwd_copy(n, b, fwd_send.at[0]).start()
-
-            return carry
-
-        lax.fori_loop(b * nslot, (b + 1) * nslot, send_rows, 0)
         if b == own_b:
 
             @pl.when(c == 0)
@@ -305,6 +295,7 @@
 
     lax.fori_loop(0, wide_d // 128, turn, 0)
     swaps[2].start()
+    send_batch(1)
 
     wgu[pl.ds(wide_d, pad), :] = jnp.zeros((pad, 4 * hid), BF16)
     wdt[pl.ds(0, pad), :] = jnp.zeros((pad, 2 * hid), BF16)
@@ -360,13 +351,16 @@
     half = nz // 2
     hops = [[half, nz - 1 - half], [nz - 1 - half, half]]
 
-    def ag_copy(b, way, s):
+    fold = -(-rows // 32) * 16
+    cuts = [pl.ds(0, fold), pl.ds(fold, rows - fold)]
+
+    def ag_copy(b, way, s, part):
         which = lax.rem(z + nz - s, nz) if way == 0 else lax.rem(z + s, nz)
         return pltpu.make_async_remote_copy(
-            src_ref=ag.at[b, which],
-            dst_ref=ag.at[b, which],
-            send_sem=ag_send.at[b, way, s],
-            recv_sem=ag_recv.at[b, way, s],
+            src_ref=ag.at[b, which, cuts[part], :],
+            dst_ref=ag.at[b, which, cuts[part], :],
+            send_sem=ag_send.at[b, way, s, part],
+            recv_sem=ag_recv.at[b, way, s, part],
             device_id=right if way == 0 else left,
             device_id_type=MESH,
         )
@@ -385,34 +379,39 @@
         acc_gu[b] += dot(first, wgu[at, :])
         acc_b[b] += dot(second, wdt[at, :])
 
-    def ag_wait(b, way, s):
-        if s < hops[b][way]:
-            ag_copy(b, way, s).wait_recv()
-
-    def ag_start(b, way, s):
-        if s < hops[b][way]:
-            ag_copy(b, way, s).start()
+    def ag_start(b, way):
+        if hops[b][way] > 0:
+            for part in range(2):
+                ag_copy(b, way, 0, part).start()
+
+    def ag_pass(*which):
+        for part in range(2):
+            for b, way, s in which:
+                if s < hops[b][way]:
+                    ag_copy(b, way, s, part).wait_recv()
+                    if s + 1 < hops[b][way]:
+                        ag_copy(b, way, s + 1, part).start()
 
     def ag_use(b, way, s):
         if s < hops[b][way]:
             multiply(b, lax.rem(z + nz - s - 1, nz) if way == 0 else lax.rem(z + s + 1, nz))
 
-    def rs_copy(b, way, s):
+    tiles = WIDE // 128 - 1
+    again_at = rows - fold
+    halves = [pl.ds(0, 2 * rows), pl.ds(2 * rows, rs_snd.shape[3] - 2 * rows)]
+
+    def rs_copy(b, way, s, part):
         return pltpu.make_async_remote_copy(
-            src_ref=rs_snd.at[b, way, s],
-            dst_ref=rs_rcv.at[b, way, s],
-            send_sem=rs_send.at[b, way, s],
-            recv_sem=rs_recv.at[b, way, s],
+            src_ref=rs_snd.at[b, way, s, halves[part], :],
+            dst_ref=rs_rcv.at[b, way, s, halves[part], :],
+            send_sem=rs_send.at[b, way, s, part],
+            recv_sem=rs_recv.at[b, way, s, part],
             device_id=right if way == 0 else left,
             device_id_type=MESH,
         )
 
     def term(b, which):
         return dot_nt(dgu[b], wgu[pl.ds(pl.multiple_of(which * chunk, pad), WIDE), :])
-
-    tiles = WIDE // 128 - 1
-    fold = rs_snd.shape[3] - tiles * rows
-    again_at = rows - fold
 
     def folded(total):
         tail = total[:, tiles * 128 :]
@@ -425,17 +424,18 @@
         for way in ways:
             over = hops[b][way] - s
             totals.append(term(b, lax.rem(z + over, nz) if way == 0 else lax.rem(z + nz - over, nz)))
-        for way, total in zip(ways, totals):
-            tail = folded(total)
-            if s > 0:
-                rs_copy(b, way, s - 1).wait_recv()
-            for i in range(tiles + 1):
-                at = pl.ds(i * rows, rows if i < tiles else fold)
-                value = total[:, i * 128 : i * 128 + 128] if i < tiles else tail
+        pieces = [[total[:, i * 128 : i * 128 + 128] for i in range(tiles)] + [folded(total)] for total in totals]
+        for part in range(2):
+            for way, piece in zip(ways, pieces):
                 if s > 0:
-                    value = value + rs_rcv[b, way, s - 1, at, :].astype(F32)
-                rs_snd[b, way, s, at, :] = value.astype(BF16)
-            rs_copy(b, way, s).start()
+                    rs_copy(b, way, s - 1, part).wait_recv()
+                for i in (2 * part, 2 * part + 1):
+                    at = pl.ds(i * rows, rows if i < tiles else fold)
+                    value = piece[i]
+                    if s > 0:
+                        value = value + rs_rcv[b, way, s - 1, at, :].astype(F32)
+                    rs_snd[b, way, s, at, :] = value.astype(BF16)
+                rs_copy(b, way, s, part).start()
 
     def middle(b):
         gate, upper = acc_gu[b, :, pl.ds(0, 2 * hid)], acc_gu[b, :, pl.ds(2 * hid, 2 * hid)]
@@ -468,9 +468,8 @@
         )
 
     build(0)
-    ag_start(0, 0, 0)
-    ag_start(0, 1, 0)
-    send_batch(1)
+    ag_start(0, 0)
+    ag_start(0, 1)
     scores[z] = jnp.zeros(scores.shape[1:], F32)
     lax.fori_loop(0, 2, set_away, 0)
     loads[7].wait()
@@ -480,35 +479,29 @@
     multiply(0, z)
 
     for s in range(half):
-        for way in range(2):
-            ag_wait(0, way, s)
-            ag_start(0, way, s + 1)
+        ag_pass((0, 0, s), (0, 1, s))
         if s == 0:
             ag_use(0, 0, s)
             ag_use(0, 1, s)
             build(1)
         if s == max(half - 3, 0):
-            ag_start(1, 1, 0)
+            ag_start(1, 1)
         if s == max(half - 2, 0):
-            ag_start(1, 0, 0)
+            ag_start(1, 0)
         if s == 0:
             multiply(1, z)
         else:
             if s == half - 1:
-                ag_wait(1, 1, 0)
-                ag_start(1, 1, 1)
+                ag_pass((1, 1, 0))
             ag_use(0, 0, s)
             ag_use(0, 1, s)
     if half == 1:
-        ag_wait(1, 1, 0)
+        ag_pass((1, 1, 0))
     middle(0)
     rs_step(0, 0)
     ag_use(1, 1, 0)
     for i in range(half - 1):
-        ag_wait(1, 0, i)
-        ag_start(1, 0, i + 1)
-        ag_wait(1, 1, i + 1)
-        ag_start(1, 1, i + 2)
+        ag_pass((1, 0, i), (1, 1, i + 1))
         if i == 0:
             set_scores(0)
         ag_use(1, 0, i)
@@ -534,10 +527,9 @@
         score = score + scores[k]
 
     def ret_copy(b, i, h, sem):
-        p, dx, home = home_of(b * nb + i)
-        n = p * NX + dx
+        n, home = home_of(b * nb + i)
         return pltpu.make_async_remote_copy(
-            src_ref=ret_snd.at[b, h, pl.ds(pl.multiple_of(i * MAIN, MAIN), MAIN), :],
+            src_ref=ret_snd.at[b, h, pl.ds(i * MAIN, MAIN), :],
             dst_ref=ret_rcv.at[pl.ds(pl.multiple_of(n * MAIN, MAIN), MAIN), :],
             send_sem=sem,
             recv_sem=ret_recv.at[b],
@@ -549,13 +541,14 @@
         total = term(b, z)
         tail = folded(total)
         parts = [total[:, i * 128 : i * 128 + 128] for i in range(tiles)] + [tail]
-        for way in range(2):
-            if hops[b][way] > 0:
-                s = hops[b][way] - 1
-                rs_copy(b, way, s).wait_recv()
-                for i in range(tiles + 1):
-                    at = pl.ds(i * rows, rows if i < tiles else fold)
-                    parts[i] = parts[i] + rs_rcv[b, way, s, at, :].astype(F32)
+        for part in range(2):
+            for way in range(2):
+                if hops[b][way] > 0:
+                    s = hops[b][way] - 1
+                    rs_copy(b, way, s, part).wait_recv()
+                    for i in (2 * part, 2 * part + 1):
+                        at = pl.ds(i * rows, rows if i < tiles else fold)
+                        parts[i] = parts[i] + rs_rcv[b, way, s, at, :].astype(F32)
         tail = parts.pop()
         lane = iota((rows, 128), 1)
         tail = jnp.concatenate([tail, pltpu.roll(tail, pad, 1)[fold - again_at :]], axis=0)
@@ -594,20 +587,16 @@
                 dot(whole, away[h, pl.ds(0, WIDE), :]) + dot(ends, away[h, pl.ds(WIDE, WIDE), :]) + carried
             ).astype(BF16)
 
-        def send_back(i, carry, b=b):
+        for i in range(nb):
             for h in range(2):
-                own = jnp.logical_and(c == 0, i == own_slot) if (b == own_b and h == 0) else None
-                if own is None:
+
+                def away_go(b=b, i=i, h=h):
                     ret_copy(b, i, h, ret_send.at[0]).start()
+
+                if (b, i, h) == (own_b, own_slot, 0):
+                    pl.when(c == 1)(away_go)
                 else:
-
-                    @pl.when(jnp.logical_not(own))
-                    def _():
-                        ret_copy(b, i, h, ret_send.at[0]).start()
-
-            return carry
-
-        lax.fori_loop(0, nb, send_back, 0)
+                    away_go()
         if b == own_b:
 
             @pl.when(c == 0)
@@ -661,8 +650,9 @@
     for b in range(2):
         for way in range(2):
             for s in range(hops[b][way]):
-                ag_copy(b, way, s).wait_send()
-                rs_copy(b, way, s).wait_send()
+                for part in range(2):
+                    ag_copy(b, way, s, part).wait_send()
+                    rs_copy(b, way, s, part).wait_send()
     for k in range(1, nz):
         sc_copy(k).wait_send()
     part = ret_rcv.at[pl.ds(0, most * MAIN), :]
@@ -724,10 +714,10 @@
             dma((3,)),
             dma((2,)),
             dma((2,)),
-            dma((2, 2, half)),
-            dma((2, 2, half)),
-            dma((2, 2, half)),
-            dma((2, 2, half)),
+            dma((2, 2, half, 2)),
+            dma((2, 2, half, 2)),
+            dma((2, 2, half, 2)),
+            dma((2, 2, half, 2)),
             dma((nz,)),
             dma((nz,)),
             dma((1,)),

time: 111 us -> 106 us (0.955)
  Pallas kernels: 109 us -> 103 us
    pallas_call x1, Pallas kernels: 109 us -> 103 us  [on_device(): pl.pallas_call(functools.partial(kernel, ny, nz), out_shape=(jax.ShapeDty...]
where the time goes in v3:
time: 106 us
  Pallas kernels  103 us (97%)
  local copies, waits for them, and re-layouts  2.03 us (2%)
    pallas_call x1, Pallas kernels, on_device(): pl.pallas_call(functools.partial(kernel, ny, nz), out_shape=(jax.ShapeDty...  103 us

profile of v3, /device:TPU:1, one launch (start us, length us, event | category | flops | bytes accessed | tf_op | source)
XLA Modules:
  0.0 105.8 jit_solution(7422651132238657533)
XLA Ops:
  0.6 103.2 %shard_map.86 = (bf16[224,128]{1,0:T(8,128)(2,1)}, f32[4,128]{1,0:T(4,128)}) custom-call(bf16[224,128]{1,0:T(8,128)(2,1)} %bitcast.13, bf16[224,128]{1,0:T(8,128)(2,1)} %bitcast.14, f32[4,128]{1,0:T(4,128)} %bitcast.16, s32[4,128]{1,0:T(4,128)} %bitcast.17, bf16[3584,128]{1,0:T(8,128)(2,1)} %bitcast.9, bf16[3584,128]{1,0:T(8,128)(2,1)} %bitcast.10, ...), custom_call_target="tpu_custom_call" | custom-call | tf_op jit(solution)/shard_map/pallas_call | solution.py:684
  103.8 0.0 copy-start
  103.8 1.4 %copy.11 = bf16[128,224]{0,1:T(8,128)(2,1)} copy(bf16[128,224]{0,1:T(8,128)(2,1)} %bitcast.12) | data formatting | bytes 114688
  105.2 0.0 copy-done
  105.2 0.6 copy.12
Async XLA Ops:
  103.8 1.5 %copy-start = (f32[4,128]{1,0:T(4,128)S(1)}, f32[4,128]{1,0:T(4,128)}, u32[]{:S(2)}) copy-start(f32[4,128]{1,0:T(4,128)} %get-tuple-element.5) | copy-start | bytes 6148

commit v4 on v3

--- a/solution.py
+++ b/solution.py
@@ -478,47 +478,42 @@
         copy.wait_recv()
     multiply(0, z)
 
-    for s in range(half):
+    ag_pass((0, 0, 0), (0, 1, 0))
+    ag_use(0, 0, 0)
+    ag_use(0, 1, 0)
+    build(1)
+    ag_start(1, 0)
+    ag_start(1, 1)
+    multiply(1, z)
+    for s in range(1, half):
         ag_pass((0, 0, s), (0, 1, s))
-        if s == 0:
-            ag_use(0, 0, s)
-            ag_use(0, 1, s)
-            build(1)
-        if s == max(half - 3, 0):
-            ag_start(1, 1)
-        if s == max(half - 2, 0):
-            ag_start(1, 0)
-        if s == 0:
-            multiply(1, z)
-        else:
-            if s == half - 1:
-                ag_pass((1, 1, 0))
-            ag_use(0, 0, s)
-            ag_use(0, 1, s)
-    if half == 1:
-        ag_pass((1, 1, 0))
+        ag_use(0, 0, s)
+        ag_use(0, 1, s)
+        if s < half - 1:
+            ag_pass((1, 0, s - 1), (1, 1, s - 1))
+            ag_use(1, 0, s - 1)
+            ag_use(1, 1, s - 1)
     middle(0)
     rs_step(0, 0)
-    ag_use(1, 1, 0)
-    for i in range(half - 1):
-        ag_pass((1, 0, i), (1, 1, i + 1))
-        if i == 0:
+    for s in range(max(half - 2, 0), half):
+        ag_pass((1, 0, s), (1, 1, s))
+        ag_use(1, 0, s)
+        ag_use(1, 1, s)
+        if s == half - 2:
             set_scores(0)
-        ag_use(1, 0, i)
-        ag_use(1, 1, i + 1)
-        if i < half - 2:
-            rs_step(0, i + 1)
+    if half == 1:
+        set_scores(0)
     middle(1)
     rs_step(1, 0)
     if half > 1:
-        rs_step(0, half - 1)
-    else:
-        set_scores(0)
+        rs_step(0, 1)
     set_scores(1)
     for k in range(1, nz):
         sc_copy(k).start()
     for s in range(1, half):
         rs_step(1, s)
+        if s + 1 < half:
+            rs_step(0, s + 1)
 
     for k in range(1, nz):
         sc_copy(k).wait_recv()

time: 106 us -> 110 us (1.038)
  Pallas kernels: 103 us -> 107 us
    pallas_call x1, Pallas kernels: 103 us -> 107 us  [on_device(): pl.pallas_call(functools.partial(kernel, ny, nz), out_shape=(jax.ShapeDty...]
where the time goes in v4:
time: 110 us
  Pallas kernels  107 us (97%)
  local copies, waits for them, and re-layouts  2.03 us (2%)
    pallas_call x1, Pallas kernels, on_device(): pl.pallas_call(functools.partial(kernel, ny, nz), out_shape=(jax.ShapeDty...  107 us

profile of v4, /device:TPU:1, one launch (start us, length us, event | category | flops | bytes accessed | tf_op | source)
XLA Modules:
  0.0 109.6 jit_solution(1884468282029068360)
XLA Ops:
  0.6 106.9 %shard_map.86 = (bf16[224,128]{1,0:T(8,128)(2,1)}, f32[4,128]{1,0:T(4,128)}) custom-call(bf16[224,128]{1,0:T(8,128)(2,1)} %bitcast.13, bf16[224,128]{1,0:T(8,128)(2,1)} %bitcast.14, f32[4,128]{1,0:T(4,128)} %bitcast.16, s32[4,128]{1,0:T(4,128)} %bitcast.17, bf16[3584,128]{1,0:T(8,128)(2,1)} %bitcast.9, bf16[3584,128]{1,0:T(8,128)(2,1)} %bitcast.10, ...), custom_call_target="tpu_custom_call" | custom-call | tf_op jit(solution)/shard_map/pallas_call | solution.py:679
  107.6 0.0 copy-start
  107.6 1.4 %copy.11 = bf16[128,224]{0,1:T(8,128)(2,1)} copy(bf16[128,224]{0,1:T(8,128)(2,1)} %bitcast.12) | data formatting | bytes 114688
  109.0 0.0 copy-done
  109.0 0.6 copy.12
Async XLA Ops:
  107.6 1.5 %copy-start = (f32[4,128]{1,0:T(4,128)S(1)}, f32[4,128]{1,0:T(4,128)}, u32[]{:S(2)}) copy-start(f32[4,128]{1,0:T(4,128)} %get-tuple-element.5) | copy-start | bytes 6148

commit v5 on v4

--- a/solution.py
+++ b/solution.py
@@ -55,7 +55,9 @@
     prob_ref,
     tt,
     snd,
+    snd_n,
     rcv,
+    rcv_n,
     place,
     away,
     hits,
@@ -78,6 +80,10 @@
     swap_recv,
     fwd_send,
     fwd_recv,
+    near_send,
+    near_recv,
+    nbr_send,
+    nbr_recv,
     ag_send,
     ag_recv,
     rs_send,
@@ -120,10 +126,10 @@
     loads = [
         pltpu.make_async_copy(ids_hbm, ids_ref, load_sem.at[0]),
         pltpu.make_async_copy(prob_hbm, prob_ref, load_sem.at[1]),
-        pltpu.make_async_copy(x_hbm, tt.at[0, pl.ds(0, feats), :], load_sem.at[2]),
-        pltpu.make_async_copy(u_hbm, tt.at[0, pl.ds(feats, feats), :], load_sem.at[3]),
-        pltpu.make_async_copy(x_hbm, tt.at[1, pl.ds(pad, feats), :], load_sem.at[4]),
-        pltpu.make_async_copy(u_hbm, tt.at[1, pl.ds(pad + feats, feats), :], load_sem.at[5]),
+        pltpu.make_async_copy(x_hbm, tt.at[0, 0, pl.ds(0, feats), :], load_sem.at[2]),
+        pltpu.make_async_copy(u_hbm, tt.at[0, 0, pl.ds(feats, feats), :], load_sem.at[3]),
+        pltpu.make_async_copy(x_hbm, tt.at[0, 1, pl.ds(pad, feats), :], load_sem.at[4]),
+        pltpu.make_async_copy(u_hbm, tt.at[0, 1, pl.ds(pad + feats, feats), :], load_sem.at[5]),
         pltpu.make_async_copy(wd_hbm, wdraw, load_sem.at[6]),
         pltpu.make_async_copy(wg_hbm, wgu.at[pl.ds(0, wide_d), pl.ds(0, hid)], load_sem.at[7]),
         pltpu.make_async_copy(wu_hbm, wgu.at[pl.ds(0, wide_d), pl.ds(2 * hid, hid)], load_sem.at[8]),
@@ -154,8 +160,9 @@
     greeted = ngroup + nslot + nz - 1 - (1 - c)
 
     zero = jnp.zeros((pad, toks), BF16)
-    tt[0, pl.ds(chunk, pad), :] = zero
-    tt[1, pl.ds(0, pad), :] = zero
+    for k in range(3):
+        tt[k, 0, pl.ds(chunk, pad), :] = zero
+        tt[k, 1, pl.ds(0, pad), :] = zero
 
     n_col = iota((ngroup, 1), 0)
     p_col = lax.shift_right_logical(n_col, 2)
@@ -182,7 +189,7 @@
 
     step_rows = min(8, ngroup // 2) * MAIN
 
-    def fill(i, carry):
+    def fill(k, i, to, first):
         base = pl.multiple_of(i * step_rows, step_rows)
         row = iota((step_rows, 1), 0)
         rr = jnp.bitwise_and(row, MAIN - 1)
@@ -193,15 +200,16 @@
         m2 = at == jnp.broadcast_to((MAIN + jnp.bitwise_and(rr, 1)).astype(F32), at.shape)
         pick1 = flag(m1)
         pickx = flag(m2)
-        pick[pl.ds(base, step_rows), :] = pick1
-        pick2[pl.ds(base, step_rows), :] = pickx
+        if k == 0:
+            pick[pl.ds(base, step_rows), :] = pick1
+            pick2[pl.ds(base, step_rows), :] = pickx
         pr1 = jnp.sum(jnp.where(m1, pr, 0.0), axis=1, keepdims=True)
         pr2 = jnp.sum(jnp.where(m2, pr, 0.0), axis=1, keepdims=True)
-        got = dot_nt(pick1, tt[0])
+        got = dot_nt(pick1, tt[k, 0])
         lane = iota((step_rows, WIDE), 1)
         got = jnp.where(jnp.logical_and(lane >= feats, lane < chunk), got * pr1, got)
-        odd = dot_nt(pickx, tt[0])
-        even = dot_nt(pickx, tt[1])
+        odd = dot_nt(pickx, tt[k, 0])
+        even = dot_nt(pickx, tt[k, 1])
         part = lax.shift_right_logical(rr, 1)
         extra = jnp.zeros((step_rows, 128), F32)
         for tile in range(WIDE // 128):
@@ -210,52 +218,76 @@
             extra = jnp.where(part == 2 * tile + 1, odd[:, cut], extra)
         lane = iota((step_rows, 128), 1)
         extra = jnp.where(part * pad + lane - (128 - pad) >= feats, extra * pr2, extra)
-        snd[pl.ds(base, step_rows), pl.ds(0, WIDE - 128)] = got[:, : WIDE - 128].astype(BF16)
-        snd[pl.ds(base, step_rows), pl.ds(WIDE - 128, 128)] = jnp.where(
+        to[pl.ds(base, step_rows), pl.ds(first, WIDE - 128)] = got[:, : WIDE - 128].astype(BF16)
+        to[pl.ds(base, step_rows), pl.ds(first + WIDE - 128, 128)] = jnp.where(
             lane >= 128 - pad, extra, got[:, WIDE - 128 :]
         ).astype(BF16)
-        return carry
+
+    steps = ngroup * MAIN // step_rows
+
+    def fill_batch(b, k):
+        def one(i, carry):
+            fill(k, i, snd if k == 0 else snd_n, 0 if k < 2 else WIDE)
+            return carry
+
+        lax.fori_loop(b * (steps // 2), (b + 1) * (steps // 2), one, 0)
 
     for copy in loads[2:6]:
         copy.wait()
-    steps = ngroup * MAIN // step_rows
-    lax.fori_loop(0, steps // 2, fill, 0)
+    fill_batch(0, 0)
     pl.semaphore_wait(barrier, greeted)
 
-    def fwd_copy(n, b, sem):
+    right = {"group": g, "dev": lax.rem(z + 1, nz) * 2 + c}
+    left = {"group": g, "dev": lax.rem(z + nz - 1, nz) * 2 + c}
+    mine = tt.at[0, 0, pl.ds(0, chunk), :]
+    near = [
+        pltpu.make_async_remote_copy(
+            src_ref=mine,
+            dst_ref=tt.at[k, 0, pl.ds(0, chunk), :],
+            send_sem=near_send.at[k - 1],
+            recv_sem=near_recv.at[k - 1],
+            device_id=right if k == 1 else left,
+            device_id_type=MESH,
+        )
+        for k in (1, 2)
+    ]
+    for copy in near:
+        copy.start()
+
+    def fwd_copy(n, b, sem, wide=False):
         p, dx, e = target(n)
         slot = p * 2 + dx // 2 - b * nb
         return pltpu.make_async_remote_copy(
-            src_ref=snd.at[pl.ds(n * MAIN, MAIN), :],
-            dst_ref=rcv.at[b, c, pl.ds(slot * MAIN, MAIN), :],
+            src_ref=(snd_n if wide else snd).at[pl.ds(n * MAIN, MAIN), :],
+            dst_ref=(rcv_n if wide else rcv).at[b, c, pl.ds(slot * MAIN, MAIN), :],
             send_sem=sem,
-            recv_sem=fwd_recv.at[b],
+            recv_sem=(nbr_recv if wide else fwd_recv).at[b],
             device_id={"group": e, "dev": z * 2 + dx % 2},
             device_id_type=MESH,
         )
 
     own_b, own_slot = (0, NX // 2) if ny > 2 else (1, 0)
 
-    def send_batch(b):
+    def send_batch(b, wide=False):
+        sem = nbr_send if wide else fwd_send
         for n in range(b * nslot, (b + 1) * nslot):
             if n != NX:
-                fwd_copy(n, b, fwd_send.at[0]).start()
+                fwd_copy(n, b, sem.at[0], wide).start()
         if b == own_b:
 
             @pl.when(c == 0)
             def _():
                 pltpu.make_async_copy(
-                    snd.at[pl.ds(NX * MAIN, MAIN), :],
-                    rcv.at[own_b, 0, pl.ds(own_slot * MAIN, MAIN), :],
-                    fwd_recv.at[own_b],
+                    (snd_n if wide else snd).at[pl.ds(NX * MAIN, MAIN), :],
+                    (rcv_n if wide else rcv).at[own_b, 0, pl.ds(own_slot * MAIN, MAIN), :],
+                    (nbr_recv if wide else fwd_recv).at[own_b],
                 ).start()
 
             @pl.when(c == 1)
             def _():
-                fwd_copy(NX, own_b, fwd_send.at[1]).start()
+                fwd_copy(NX, own_b, sem.at[1], wide).start()
 
     send_batch(0)
-    lax.fori_loop(steps // 2, steps, fill, 0)
 
     swaps = [
         pltpu.make_async_remote_copy(
@@ -285,6 +317,7 @@
     ]
     swaps[0].start()
     swaps[1].start()
+    fill_batch(1, 0)
 
     loads[6].wait()
 
@@ -295,6 +328,15 @@
 
     lax.fori_loop(0, wide_d // 128, turn, 0)
     swaps[2].start()
+
+    for copy in near:
+        copy.wait_recv()
+    for k in (1, 2):
+        tt[k, 1, pl.ds(pad, chunk), :] = tt[k, 0, pl.ds(0, chunk), :]
+    for b in range(2):
+        for k in (1, 2):
+            fill_batch(b, k)
+        send_batch(b, True)
     send_batch(1)
 
     wgu[pl.ds(wide_d, pad), :] = jnp.zeros((pad, 4 * hid), BF16)
@@ -325,6 +367,16 @@
 
     def build(b):
         pltpu.make_async_copy(rcv.at[b], rcv.at[b], fwd_recv.at[b]).wait()
+        arrange(b, z, rcv, 0)
+
+    def build_next(b):
+        pltpu.make_async_copy(rcv_n.at[b], rcv_n.at[b], nbr_recv.at[b]).wait()
+        arrange(b, before, rcv_n, 0)
+        arrange(b, after, rcv_n, WIDE)
+
+    before, after = lax.rem(z + nz - 1, nz), lax.rem(z + 1, nz)
+
+    def arrange(b, which, came, first):
         widen = flag(iota((128, WIDE), 0) == 128 - pad + jnp.bitwise_and(iota((128, WIDE), 1), pad - 1))
         mine = lax.shift_right_logical(jnp.bitwise_and(iota((main, WIDE), 0), MAIN - 1), 1) == lax.shift_right_logical(
             iota((main, WIDE), 1), pad.bit_length() - 1
@@ -338,24 +390,23 @@
         )
         whole, extra = 0.0, 0.0
         for h in range(2):
-            got = rcv[b, h]
+            got = came[b, h, :, pl.ds(first, WIDE)]
             wide = jnp.where(mine, dot(got[:, WIDE - 128 :], widen), 0.0).astype(BF16)
             last = dot(gather, wide).astype(BF16)
             whole = whole + dot(got, place[h])
             extra = extra + dot(last, place[h])
-        ag[b, z, pl.ds(0, main), :] = whole.astype(BF16)
-        ag[b, z, pl.ds(main, 2 * nb), :] = extra.astype(BF16)
-
-    right = {"group": g, "dev": lax.rem(z + 1, nz) * 2 + c}
-    left = {"group": g, "dev": lax.rem(z + nz - 1, nz) * 2 + c}
+        ag[b, which, pl.ds(0, main), :] = whole.astype(BF16)
+        ag[b, which, pl.ds(main, 2 * nb), :] = extra.astype(BF16)
+
     half = nz // 2
     hops = [[half, nz - 1 - half], [nz - 1 - half, half]]
+    ag_hops = [[half - 1, half - 2], [half - 2, half - 1]]
 
     fold = -(-rows // 32) * 16
     cuts = [pl.ds(0, fold), pl.ds(fold, rows - fold)]
 
     def ag_copy(b, way, s, part):
-        which = lax.rem(z + nz - s, nz) if way == 0 else lax.rem(z + s, nz)
+        which = lax.rem(z + 2 * nz - 1 - s, nz) if way == 0 else lax.rem(z + 1 + s, nz)
         return pltpu.make_async_remote_copy(
             src_ref=ag.at[b, which, cuts[part], :],
             dst_ref=ag.at[b, which, cuts[part], :],
@@ -380,21 +431,21 @@
         acc_b[b] += dot(second, wdt[at, :])
 
     def ag_start(b, way):
-        if hops[b][way] > 0:
+        if ag_hops[b][way] > 0:
             for part in range(2):
                 ag_copy(b, way, 0, part).start()
 
     def ag_pass(*which):
         for part in range(2):
             for b, way, s in which:
-                if s < hops[b][way]:
+                if s < ag_hops[b][way]:
                     ag_copy(b, way, s, part).wait_recv()
-                    if s + 1 < hops[b][way]:
+                    if s + 1 < ag_hops[b][way]:
                         ag_copy(b, way, s + 1, part).start()
 
     def ag_use(b, way, s):
-        if s < hops[b][way]:
-            multiply(b, lax.rem(z + nz - s - 1, nz) if way == 0 else lax.rem(z + s + 1, nz))
+        if s < ag_hops[b][way]:
+            multiply(b, lax.rem(z + 2 * nz - s - 2, nz) if way == 0 else lax.rem(z + s + 2, nz))
 
     tiles = WIDE // 128 - 1
     again_at = rows - fold
@@ -467,42 +518,45 @@
             device_id_type=MESH,
         )
 
-    build(0)
+    build_next(0)
     ag_start(0, 0)
     ag_start(0, 1)
+    build(0)
     scores[z] = jnp.zeros(scores.shape[1:], F32)
     lax.fori_loop(0, 2, set_away, 0)
     loads[7].wait()
     loads[8].wait()
     for copy in swaps:
         copy.wait_recv()
-    multiply(0, z)
-
+    for which in (z, before, after):
+        multiply(0, which)
+
+    last = half - 1
     ag_pass((0, 0, 0), (0, 1, 0))
     ag_use(0, 0, 0)
     ag_use(0, 1, 0)
-    build(1)
+    build_next(1)
     ag_start(1, 0)
     ag_start(1, 1)
-    multiply(1, z)
-    for s in range(1, half):
+    build(1)
+    for which in (z, before, after):
+        multiply(1, which)
+    for s in range(1, last):
         ag_pass((0, 0, s), (0, 1, s))
         ag_use(0, 0, s)
         ag_use(0, 1, s)
-        if s < half - 1:
+        if s < last - 1:
             ag_pass((1, 0, s - 1), (1, 1, s - 1))
             ag_use(1, 0, s - 1)
             ag_use(1, 1, s - 1)
     middle(0)
     rs_step(0, 0)
-    for s in range(max(half - 2, 0), half):
+    for s in range(max(last - 2, 0), last):
         ag_pass((1, 0, s), (1, 1, s))
         ag_use(1, 0, s)
         ag_use(1, 1, s)
-        if s == half - 2:
+        if s == max(last - 2, 0):
             set_scores(0)
-    if half == 1:
-        set_scores(0)
     middle(1)
     rs_step(1, 0)
     if half > 1:
@@ -640,14 +694,18 @@
     most = 2 * nslot - 1
     part = snd.at[pl.ds(0, most * MAIN), :]
     pltpu.make_async_copy(part, part, fwd_send.at[0]).wait()
-    for copy in swaps:
+    part = snd_n.at[pl.ds(0, most * MAIN), :]
+    pltpu.make_async_copy(part, part, nbr_send.at[0]).wait()
+    for copy in swaps + near:
         copy.wait_send()
     for b in range(2):
         for way in range(2):
             for s in range(hops[b][way]):
                 for part in range(2):
+                    rs_copy(b, way, s, part).wait_send()
+            for s in range(ag_hops[b][way]):
+                for part in range(2):
                     ag_copy(b, way, s, part).wait_send()
-                    rs_copy(b, way, s, part).wait_send()
     for k in range(1, nz):
         sc_copy(k).wait_send()
     part = ret_rcv.at[pl.ds(0, most * MAIN), :]
@@ -657,6 +715,8 @@
     def _():
         one = snd.at[pl.ds(0, MAIN), :]
         pltpu.make_async_copy(one, one, fwd_send.at[1]).wait()
+        one = snd_n.at[pl.ds(0, MAIN), :]
+        pltpu.make_async_copy(one, one, nbr_send.at[1]).wait()
         one = ret_rcv.at[pl.ds(0, MAIN), :]
         pltpu.make_async_copy(one, one, ret_send.at[0]).wait()
 
@@ -684,9 +744,11 @@
         scratch_shapes=[
             pltpu.VMEM((top, toks), I32),
             pltpu.VMEM((top, toks), F32),
-            pltpu.VMEM((2, WIDE, toks), BF16),
+            pltpu.VMEM((3, 2, WIDE, toks), BF16),
             pltpu.VMEM((ngroup * MAIN, WIDE), BF16),
+            pltpu.VMEM((ngroup * MAIN, 2 * WIDE), BF16),
             pltpu.VMEM((2, 2, main, WIDE), BF16),
+            pltpu.VMEM((2, 2, main, 2 * WIDE), BF16),
             pltpu.VMEM((2, WIDE, 2 * chunk), BF16),
             pltpu.VMEM((2, 2 * WIDE, BACK), BF16),
             pltpu.VMEM((ngroup, toks), F32),
@@ -709,6 +771,10 @@
             dma((3,)),
             dma((2,)),
             dma((2,)),
+            dma((2,)),
+            dma((2,)),
+            dma((2,)),
+            dma((2,)),
             dma((2, 2, half, 2)),
             dma((2, 2, half, 2)),
             dma((2, 2, half, 2)),

time: 110 us -> 115 us (1.045)
  Pallas kernels: 107 us -> 112 us
    pallas_call x1, Pallas kernels: 107 us -> 112 us  [on_device(): pl.pallas_call(functools.partial(kernel, ny, nz), out_shape=(jax.ShapeDty...]
where the time goes in v5:
time: 115 us
  Pallas kernels  112 us (97%)
  local copies, waits for them, and re-layouts  2.03 us (2%)
    pallas_call x1, Pallas kernels, on_device(): pl.pallas_call(functools.partial(kernel, ny, nz), out_shape=(jax.ShapeDty...  112 us

profile of v5, /device:TPU:1, one launch (start us, length us, event | category | flops | bytes accessed | tf_op | source)
XLA Modules:
  0.0 114.9 jit_solution(14404163596986467353)
XLA Ops:
  0.6 112.3 %shard_map.86 = (bf16[224,128]{1,0:T(8,128)(2,1)}, f32[4,128]{1,0:T(4,128)}) custom-call(bf16[224,128]{1,0:T(8,128)(2,1)} %bitcast.13, bf16[224,128]{1,0:T(8,128)(2,1)} %bitcast.14, f32[4,128]{1,0:T(4,128)} %bitcast.16, s32[4,128]{1,0:T(4,128)} %bitcast.17, bf16[3584,128]{1,0:T(8,128)(2,1)} %bitcast.9, bf16[3584,128]{1,0:T(8,128)(2,1)} %bitcast.10, ...), custom_call_target="tpu_custom_call" | custom-call | tf_op jit(solution)/shard_map/pallas_call | solution.py:739
  112.9 0.0 copy-start
  112.9 1.4 %copy.11 = bf16[128,224]{0,1:T(8,128)(2,1)} copy(bf16[128,224]{0,1:T(8,128)(2,1)} %bitcast.12) | data formatting | bytes 114688
  114.4 0.0 copy-done
  114.4 0.6 copy.12
Async XLA Ops:
  112.9 1.5 %copy-start = (f32[4,128]{1,0:T(4,128)S(1)}, f32[4,128]{1,0:T(4,128)}, u32[]{:S(2)}) copy-start(f32[4,128]{1,0:T(4,128)} %get-tuple-element.5) | copy-start | bytes 6148

commit v6 on v4

--- a/solution.py
+++ b/solution.py
@@ -346,8 +346,13 @@
         ag[b, z, pl.ds(0, main), :] = whole.astype(BF16)
         ag[b, z, pl.ds(main, 2 * nb), :] = extra.astype(BF16)
 
-    right = {"group": g, "dev": lax.rem(z + 1, nz) * 2 + c}
-    left = {"group": g, "dev": lax.rem(z + nz - 1, nz) * 2 + c}
+    turn_to = 1 - 2 * c
+    right = {"group": g, "dev": lax.rem(z + nz + turn_to, nz) * 2 + c}
+    left = {"group": g, "dev": lax.rem(z + nz - turn_to, nz) * 2 + c}
+
+    def along(k):
+        return lax.rem(z + 2 * nz + k * turn_to, nz)
+
     half = nz // 2
     hops = [[half, nz - 1 - half], [nz - 1 - half, half]]
 
@@ -355,7 +360,7 @@
     cuts = [pl.ds(0, fold), pl.ds(fold, rows - fold)]
 
     def ag_copy(b, way, s, part):
-        which = lax.rem(z + nz - s, nz) if way == 0 else lax.rem(z + s, nz)
+        which = along(-s) if way == 0 else along(s)
         return pltpu.make_async_remote_copy(
             src_ref=ag.at[b, which, cuts[part], :],
             dst_ref=ag.at[b, which, cuts[part], :],
@@ -394,7 +399,7 @@
 
     def ag_use(b, way, s):
         if s < hops[b][way]:
-            multiply(b, lax.rem(z + nz - s - 1, nz) if way == 0 else lax.rem(z + s + 1, nz))
+            multiply(b, along(-s - 1) if way == 0 else along(s + 1))
 
     tiles = WIDE // 128 - 1
     again_at = rows - fold
@@ -423,7 +428,7 @@
         totals = []
         for way in ways:
             over = hops[b][way] - s
-            totals.append(term(b, lax.rem(z + over, nz) if way == 0 else lax.rem(z + nz - over, nz)))
+            totals.append(term(b, along(over) if way == 0 else along(-over)))
         pieces = [[total[:, i * 128 : i * 128 + 128] for i in range(tiles)] + [folded(total)] for total in totals]
         for part in range(2):
             for way, piece in zip(ways, pieces):

time: 110 us -> 105 us (0.955)
  Pallas kernels: 107 us -> 102 us
    pallas_call x1, Pallas kernels: 107 us -> 102 us  [on_device(): pl.pallas_call(functools.partial(kernel, ny, nz), out_shape=(jax.ShapeDty...]
where the time goes in v6:
time: 105 us; the launch traced here: 104 us
  Pallas kernels  102 us (97%)
  local copies, waits for them, and re-layouts  2.03 us (2%)
    pallas_call x1, Pallas kernels, on_device(): pl.pallas_call(functools.partial(kernel, ny, nz), out_shape=(jax.ShapeDty...  102 us

profile of v6, /device:TPU:1, one launch (start us, length us, event | category | flops | bytes accessed | tf_op | source)
XLA Modules:
  0.0 104.4 jit_solution(17217472155186225132)
XLA Ops:
  0.6 101.7 %shard_map.86 = (bf16[224,128]{1,0:T(8,128)(2,1)}, f32[4,128]{1,0:T(4,128)}) custom-call(bf16[224,128]{1,0:T(8,128)(2,1)} %bitcast.13, bf16[224,128]{1,0:T(8,128)(2,1)} %bitcast.14, f32[4,128]{1,0:T(4,128)} %bitcast.16, s32[4,128]{1,0:T(4,128)} %bitcast.17, bf16[3584,128]{1,0:T(8,128)(2,1)} %bitcast.9, bf16[3584,128]{1,0:T(8,128)(2,1)} %bitcast.10, ...), custom_call_target="tpu_custom_call" | custom-call | tf_op jit(solution)/shard_map/pallas_call | solution.py:684
  102.3 0.0 copy-start
  102.3 1.4 %copy.11 = bf16[128,224]{0,1:T(8,128)(2,1)} copy(bf16[128,224]{0,1:T(8,128)(2,1)} %bitcast.12) | data formatting | bytes 114688
  103.8 0.0 copy-done
  103.8 0.6 copy.12
Async XLA Ops:
  102.3 1.5 %copy-start = (f32[4,128]{1,0:T(4,128)S(1)}, f32[4,128]{1,0:T(4,128)}, u32[]{:S(2)}) copy-start(f32[4,128]{1,0:T(4,128)} %get-tuple-element.5) | copy-start | bytes 6148

commit v7 on v6

--- a/solution.py
+++ b/solution.py
@@ -256,6 +256,7 @@
 
     send_batch(0)
     lax.fori_loop(steps // 2, steps, fill, 0)
+    send_batch(1)
 
     swaps = [
         pltpu.make_async_remote_copy(
@@ -295,7 +296,6 @@
 
     lax.fori_loop(0, wide_d // 128, turn, 0)
     swaps[2].start()
-    send_batch(1)
 
     wgu[pl.ds(wide_d, pad), :] = jnp.zeros((pad, 4 * hid), BF16)
     wdt[pl.ds(0, pad), :] = jnp.zeros((pad, 2 * hid), BF16)
@@ -483,31 +483,24 @@
         copy.wait_recv()
     multiply(0, z)
 
-    ag_pass((0, 0, 0), (0, 1, 0))
-    ag_use(0, 0, 0)
-    ag_use(0, 1, 0)
     build(1)
     ag_start(1, 0)
     ag_start(1, 1)
     multiply(1, z)
-    for s in range(1, half):
+    for s in range(half):
         ag_pass((0, 0, s), (0, 1, s))
         ag_use(0, 0, s)
         ag_use(0, 1, s)
         if s < half - 1:
-            ag_pass((1, 0, s - 1), (1, 1, s - 1))
-            ag_use(1, 0, s - 1)
-            ag_use(1, 1, s - 1)
+            ag_pass((1, 0, s), (1, 1, s))
+            ag_use(1, 0, s)
+            ag_use(1, 1, s)
     middle(0)
     rs_step(0, 0)
-    for s in range(max(half - 2, 0), half):
-        ag_pass((1, 0, s), (1, 1, s))
-        ag_use(1, 0, s)
-        ag_use(1, 1, s)
-        if s == half - 2:
-            set_scores(0)
-    if half == 1:
-        set_scores(0)
+    ag_pass((1, 0, half - 1), (1, 1, half - 1))
+    ag_use(1, 0, half - 1)
+    ag_use(1, 1, half - 1)
+    set_scores(0)
     middle(1)
     rs_step(1, 0)
     if half > 1:

time: 105 us -> 106 us (level)
    pallas_call x1, Pallas kernels: 102 us -> 103 us  [on_device(): pl.pallas_call(functools.partial(kernel, ny, nz), out_shape=(jax.ShapeDty...]
where the time goes in v7:
time: 106 us
  Pallas kernels  103 us (97%)
  local copies, waits for them, and re-layouts  2.03 us (2%)
    pallas_call x1, Pallas kernels, on_device(): pl.pallas_call(functools.partial(kernel, ny, nz), out_shape=(jax.ShapeDty...  103 us

profile of v7, /device:TPU:1, one launch (start us, length us, event | category | flops | bytes accessed | tf_op | source)
XLA Modules:
  0.0 105.9 jit_solution(12062398732635921073)
XLA Ops:
  0.6 103.2 %shard_map.86 = (bf16[224,128]{1,0:T(8,128)(2,1)}, f32[4,128]{1,0:T(4,128)}) custom-call(bf16[224,128]{1,0:T(8,128)(2,1)} %bitcast.13, bf16[224,128]{1,0:T(8,128)(2,1)} %bitcast.14, f32[4,128]{1,0:T(4,128)} %bitcast.16, s32[4,128]{1,0:T(4,128)} %bitcast.17, bf16[3584,128]{1,0:T(8,128)(2,1)} %bitcast.9, bf16[3584,128]{1,0:T(8,128)(2,1)} %bitcast.10, ...), custom_call_target="tpu_custom_call" | custom-call | tf_op jit(solution)/shard_map/pallas_call | solution.py:677
  103.9 0.0 copy-start
  103.9 1.4 %copy.11 = bf16[128,224]{0,1:T(8,128)(2,1)} copy(bf16[128,224]{0,1:T(8,128)(2,1)} %bitcast.12) | data formatting | bytes 114688
  105.3 0.0 copy-done
  105.3 0.6 copy.12
Async XLA Ops:
  103.9 1.5 %copy-start = (f32[4,128]{1,0:T(4,128)S(1)}, f32[4,128]{1,0:T(4,128)}, u32[]{:S(2)}) copy-start(f32[4,128]{1,0:T(4,128)} %get-tuple-element.5) | copy-start | bytes 6148
